TPU v7x, 32 devices: a whole 2x2x4 slice. The times are simulated.
32 devices in a mesh: seq: 4 (over z), tp: 4 (over y, x), lat: 2 (over core).
Axes of the slice: x: 2, y: 2, z: 4, core: 2. Of those that a mesh axis runs over, the one named last changes fastest.
Arguments:
- tokens: bfloat16 [3072, 8192], P(('seq', 'lat'), 'tp'), may hold values from -6 to 6
- active: int32 [3072, 4], P(('seq', 'lat')), may hold values from 0 to 31, all different within a row; in each aligned block of 384 rows (0 to 383, 384 to 767, ...) at most 72 rows name the same one
- placement_map: int32 [32], replicated, may hold values from 0 to 31, each once
- enc_weight: bfloat16 [8192, 4096], P('tp', ('seq', 'lat')), may hold values from -0.0625 to 0.0625
- enc_bias: float32 [4096], P(('seq', 'lat')), may hold values from -3 to 3
- dec_weight: bfloat16 [4096, 8192], P(('seq', 'lat'), 'tp'), may hold values from -0.375 to 0.375
- dec_bias: float32 [8192], P('tp'), may hold values from -3 to 3
Outputs:
- recon: bfloat16 [3072, 8192], P(('seq', 'lat'), 'tp')
Inputs may be any that keep to these rules, and one draw needn't show every extreme that they name: `active`: the 4 blocks of one token are different. Among the rows of one device (aligned blocks of 384 rows) no block is named more than 72 times, and some block is named exactly 72 times. `placement_map`: each column block appears once.
All inputs are finite; a program needn't handle non-finite values.
Results may differ from a plain program's by a relative error of at most 0.0061.
Values may be sent and summed in bfloat16 or wider, within the bound.
No kernel may reach another device: no remote copies, remote signals or barrier semaphores. Data moves between devices by JAX's collectives and lax.ppermute only.
A program may use at most 128 MiB of HBM per device.

v0:
```python
import jax
import jax.numpy as jnp
from jax import lax
from jax.sharding import PartitionSpec as P


def local(tokens, active, placement_map, enc_weight, enc_bias, dec_weight, dec_bias):
    rows, width = tokens.shape
    top = active.shape[1]
    nblocks = placement_map.shape[0]
    seq_count = lax.axis_size("seq")
    lat_count = lax.axis_size("lat")
    owners = seq_count * lat_count
    local_blocks = nblocks // owners
    block_width = enc_bias.shape[0] // local_blocks
    capacity = 3 * rows * top // (2 * nblocks)
    centered = (tokens.astype(jnp.float32) - dec_bias[None, :]).astype(jnp.bfloat16)
    block_ids = jnp.arange(nblocks, dtype=jnp.int32)
    matches = (active[:, :, None] == block_ids[None, None, :]).astype(jnp.int32)
    position = jnp.sum(matches * placement_map[None, None, :], axis=2).reshape(-1)
    pos_hot = (position[:, None] == block_ids[None, :]).astype(jnp.int32)
    rank = jnp.sum((jnp.cumsum(pos_hot, axis=0) - 1) * pos_hot, axis=1)
    target = position * capacity + rank
    pair_row = jnp.arange(rows * top, dtype=jnp.int32) // top
    slot_row = jnp.zeros((nblocks * capacity,), jnp.int32).at[target].set(pair_row)
    filled = jnp.zeros((nblocks * capacity,), jnp.bool_).at[target].set(True)
    outgoing = jnp.where(filled[:, None], centered[slot_row], jnp.zeros((), jnp.bfloat16))
    outgoing = outgoing.reshape(owners, local_blocks, capacity, width)
    enc_blocks = enc_weight.reshape(width, local_blocks, block_width)
    bias_blocks = enc_bias.reshape(local_blocks, block_width)
    dec_blocks = dec_weight.reshape(local_blocks, block_width, width)
    preact = jnp.einsum(
        "sbcd,dbh->sbch",
        lax.all_to_all(outgoing, ("seq", "lat"), split_axis=0, concat_axis=0, tiled=True),
        enc_blocks,
        preferred_element_type=jnp.float32,
    )
    summed = lax.psum(preact, "tp")
    codes = jnp.maximum(summed + bias_blocks[None, :, None, :], 0.0).astype(jnp.bfloat16)
    returned = lax.all_to_all(
        jnp.einsum("sbch,bhd->sbcd", codes, dec_blocks, preferred_element_type=jnp.float32).astype(
            jnp.bfloat16
        ),
        ("seq", "lat"),
        split_axis=0,
        concat_axis=0,
        tiled=True,
    )
    returned = returned.reshape(nblocks * capacity, width)
    contrib = returned[target].reshape(rows, top, width).astype(jnp.float32)
    return (jnp.sum(contrib, axis=1) + dec_bias[None, :]).astype(jnp.bfloat16)


def solution(mesh):
    return jax.shard_map(
        local,
        mesh=mesh,
        in_specs=(
            P(("seq", "lat"), "tp"),
            P(("seq", "lat"), None),
            P(),
            P("tp", ("seq", "lat")),
            P(("seq", "lat")),
            P(("seq", "lat"), "tp"),
            P("tp"),
        ),
        out_specs=P(("seq", "lat"), "tp"),
        check_vma=False,
    )
```

profile of v0, /device:TPU:0, one launch (start us, length us, event | category | flops | bytes accessed | tf_op | source)
XLA Modules:
  0.0 619.6 jit_solution(3013222002014021697)
XLA Ops:
  6.5 1.0 select_reduce_fusion
  7.5 0.1 copy.32
  7.7 0.1 eq.45
  7.8 0.1 eq.41
  8.0 9.1 %reduce-window.6 = s32[32,12,128]{2,1,0:T(8,128)S(1)} reduce-window(s32[32,12,128]{2,1,0:T(8,128)S(1)} %fusion.10, s32[]{:T(128)} %constant.32.clone.1), window={size=1x1x128 pad=0_0x0_0x127_0}, to_apply=%region_1.0 | reduce-window | flops 6242304 | bytes 393220 | tf_op jit(solution)/shard_map/reduce-window
  17.1 0.1 slice.12
  17.2 0.2 copy.34
  17.4 0.1 copy.35
  17.5 0.1 add_add_fusion
  17.7 0.1 copy.31
  17.8 0.2 mul.31
  18.0 0.1 fusion.12
  18.1 6.2 scatter_custom_fusion.1
  24.3 11.2 %scatter_custom_fusion = pred[2304]{0:T(1024)(128)(4,1)S(1)} fusion(s32[1536]{0:T(1024)S(1)} %fusion.16, pred[1536]{0:T(1024)(128)(4,1)S(1)} %broadcast.82, pred[]{:T(512)} %constant.16.clone.1), kind=kCustom, calls=%fused_computation.38 | custom fusion | bytes 2305 | tf_op jit(solution)/shard_map/scatter | solution.py:26
  35.5 0.1 broadcast_in_dim.35
  35.7 2.9 subtract_convert_fusion
  38.6 20.0 %gather_fusion = bf16[2304,2048]{1,0:T(8,128)(2,1)} fusion(bf16[384,2048]{1,0:T(8,128)(2,1)} %subtract_convert_fusion, s32[3072]{0:T(1024)S(1)} %pad_clamp_fusion), kind=kCustom, calls=%fused_computation | custom fusion | bytes 18883584 | tf_op jit(solution)/shard_map/gather | solution.py:27
  58.6 8.0 %broadcast_select_fusion = bf16[8,4,72,2048]{3,2,1,0:T(8,128)(2,1)} fusion(bf16[8,4,72,2048]{3,2,1,0:T(8,128)(2,1)} %bitcast.30, pred[8,4,72]{2,1,0:T(4,128)(4,1)S(1)} %broadcast_in_dim.35), kind=kLoop, calls=%fused_computation.7 | loop fusion | flops 4718592 | bytes 18876672 | tf_op jit(solution)/shard_map/jit(_where)/select_n | solution.py:27
  66.6 6.3 %all-to-all-start = ((bf16[8,4,72,2048]{3,2,1,0:T(8,128)(2,1)}), bf16[8,4,72,2048]{3,2,1,0:T(8,128)(2,1)}, u32[]{:S(2)}, u32[]{:S(2)}) async-start(bf16[8,4,72,2048]{3,2,1,0:T(8,128)(2,1)} %broadcast_select_fusion), calls=%async_computation | async-start | bytes 18874368 | tf_op jit(solution)/shard_map/all_to_all | solution.py:34
  72.9 0.2 all-reduce.2.cloned.1.call-start
  73.1 4.0 reshape.73
  77.1 202.3 %all-to-all-done = bf16[8,4,72,2048]{3,2,1,0:T(8,128)(2,1)} async-done(((bf16[8,4,72,2048]{3,2,1,0:T(8,128)(2,1)}), bf16[8,4,72,2048]{3,2,1,0:T(8,128)(2,1)}, u32[]{:S(2)}, u32[]{:S(2)}) %all-to-all-start) | async-done | bytes 9437216 | tf_op jit(solution)/shard_map/all_to_all | solution.py:34
  279.4 7.9 %fusion.3 = f32[8,4,72,128]{3,2,0,1:T(8,128)} fusion(bf16[2048,4,128,1]{2,1,0,3:T(4,128)(2,1)} %bitcast.31, bf16[8,4,72,2048]{3,2,1,0:T(8,128)(2,1)} %all-to-all-done), kind=kOutput, calls=%fused_computation.11 | convolution fusion | flops 1207959552 | bytes 12713984 | tf_op jit(solution)/shard_map/sbcd,dbh->sbch/dot_general | solution.py:32
  287.3 53.5 %all-reduce.2.cloned.1.call-done = f32[8,4,72,128]{3,2,0,1:T(8,128)} async-done(((f32[8,4,72,128]{3,2,0,1:T(8,128)}), f32[8,4,72,128]{3,2,0,1:T(8,128)}) %all-reduce.2.cloned.1.call-update) | async-done | bytes 1179664 | tf_op jit(solution)/shard_map/psum | solution.py:38
  340.9 6.4 %convert_bitcast_fusion = bf16[8,4,72,2048]{3,2,0,1:T(8,128)(2,1)} fusion(bf16[4,128,2048,1]{2,1,3,0:T(8,128)(2,1)S(1)} %bitcast.29, f32[8,4,72,128]{3,2,0,1:T(8,128)} %all-reduce.2.cloned.1.call-done, f32[4,128]{1,0:T(4,128)S(1)} %bitcast.35), kind=kOutput, calls=%fused_computation.6 | convolution fusion | flops 1213562880 | bytes 12716032 | tf_op jit(solution)/shard_map/sbch,bhd->sbcd/dot_general | solution.py:41
  347.3 9.3 %copy.38 = bf16[8,4,72,2048]{3,2,1,0:T(8,128)(2,1)} copy(bf16[8,4,72,2048]{3,2,0,1:T(8,128)(2,1)} %convert_bitcast_fusion) | data formatting | bytes 18874368 | tf_op jit(solution)/shard_map/convert_element_type | solution.py:41
  356.5 5.0 all-to-all-start.1
  361.6 206.3 %all-to-all-done.1 = bf16[8,4,72,2048]{3,2,1,0:T(8,128)(2,1)} async-done(((bf16[8,4,72,2048]{3,2,1,0:T(8,128)(2,1)}), bf16[8,4,72,2048]{3,2,1,0:T(8,128)(2,1)}, u32[]{:S(2)}, u32[]{:S(2)}) %all-to-all-start.1) | async-done | bytes 9437216 | tf_op jit(solution)/shard_map/all_to_all | solution.py:40
  567.9 17.6 %gather_fusion.1 = bf16[1536,2048]{1,0:T(8,128)(2,1)} fusion(bf16[2304,2048]{1,0:T(8,128)(2,1)} %bitcast.10, s32[2048]{0:T(1024)S(1)} %pad_clamp_fusion.1), kind=kCustom, calls=%fused_computation.1 | custom fusion | bytes 12589056 | tf_op jit(solution)/shard_map/gather | solution.py:50
  585.6 11.9 %reshape.76 = f32[384,4,2048]{2,1,0:T(4,128)} reshape(bf16[1536,2048]{1,0:T(8,128)(2,1)} %gather_fusion.1) | data formatting | bytes 18874368 | tf_op jit(solution)/shard_map/convert_element_type | solution.py:50
  597.4 11.9 %reduce_sum.32 = f32[384,2048]{1,0:T(8,128)} reduce(f32[384,4,2048]{2,1,0:T(4,128)} %reshape.76, f32[]{:T(128)} %constant.42.clone.1), dimensions={1}, to_apply=%region_7.8 | reduce | flops 2359296 | bytes 15728644 | tf_op jit(solution)/shard_map/reduce_sum | solution.py:51
  609.4 3.4 add_convert_fusion
  (18 shorter events, 0.1 us)
Async XLA Ops:
  6.5 334.4 %copy-start = (bf16[512,2048]{1,0:T(8,128)(2,1)S(1)}, bf16[512,2048]{1,0:T(8,128)(2,1)}, u32[]{:S(2)}) copy-start(bf16[512,2048]{1,0:T(8,128)(2,1)} %param.12) | copy-start | bytes 6291460
  6.5 29.1 %copy-start.2 = (f32[2048]{0:T(1024)S(1)}, f32[2048]{0:T(1024)}, u32[]{:S(2)}) copy-start(f32[2048]{0:T(1024)} %param.13) | copy-start | bytes 24580
  66.6 212.8 %all-to-all-start = ((bf16[8,4,72,2048]{3,2,1,0:T(8,128)(2,1)}), bf16[8,4,72,2048]{3,2,1,0:T(8,128)(2,1)}, u32[]{:S(2)}, u32[]{:S(2)}) async-start(bf16[8,4,72,2048]{3,2,1,0:T(8,128)(2,1)} %broadcast_select_fusion), calls=%async_computation | async-start | bytes 18874368 | tf_op jit(solution)/shard_map/all_to_all | solution.py:34
  72.9 268.0 %all-reduce.2.cloned.1.call-start = ((), (), s32[]{:S(2)}) async-start(), calls=%async_computation.2 | async-start | bytes 2359296 | tf_op jit(solution)/shard_map/psum | solution.py:38
  279.4 61.5 %copy-start.3 = (f32[512]{0:T(512)S(1)}, f32[512]{0:T(512)}, u32[]{:S(2)}) copy-start(f32[512]{0:T(512)} %param.11) | copy-start | bytes 6148
  356.5 211.4 %all-to-all-start.1 = ((bf16[8,4,72,2048]{3,2,1,0:T(8,128)(2,1)}), bf16[8,4,72,2048]{3,2,1,0:T(8,128)(2,1)}, u32[]{:S(2)}, u32[]{:S(2)}) async-start(bf16[8,4,72,2048]{3,2,1,0:T(8,128)(2,1)} %copy.38), calls=%async_computation.1 | async-start | bytes 18874368 | tf_op jit(solution)/shard_map/all_to_all | solution.py:40
  597.4 15.3 %copy-start.1 = (bf16[512,2048]{1,0:T(8,128)(2,1)S(1)}, bf16[512,2048]{1,0:T(8,128)(2,1)}, u32[]{:S(2)}) copy-start(bf16[512,2048]{1,0:T(8,128)(2,1)} %param.12) | copy-start | bytes 6291460
Sparse Core Ops, SparseCore 0:
  287.5 53.3 all-reduce.1
where the time goes:
time: 621 us; the launch traced here: 620 us
  waiting for transfers between devices  462 us (74%)
  local copies, waits for them, and re-layouts  81.3 us (13%)
  other arithmetic  36.6 us (6%)
  matrix products  14.3 us (2%)
  between operations  13.5 us (2%)
  starting transfers between devices  11.6 us (2%)
    all_to_all x1, waiting for transfers between devices, local(): lax.all_to_all(jnp.einsum('sbch,bhd->sbcd', codes, dec_blocks, preferred_...  206 us
    all_to_all x1, waiting for transfers between devices, local(): lax.all_to_all(outgoing, ('seq', 'lat'), split_axis=0, concat_axis=0, til...  202 us
    psum x1, waiting for transfers between devices, local(): summed = lax.psum(preact, 'tp')  53.5 us
    gather x1, local copies, waits for them, and re-layouts, local(): centered[slot_row]  20 us
    gather x1, local copies, waits for them, and re-layouts, local(): contrib = returned[target].reshape(rows, top, width).astype(jnp.float32)  17.6 us
  transfers between devices with their start and end apart: 3, of which 3 were waited for; matrix products, arithmetic and copies ran while one was open for 1% of the time, Pallas kernels for 0%

commit v1 on v0

--- a/solution.py
+++ b/solution.py
@@ -1,10 +1,258 @@
 import jax
 import jax.numpy as jnp
 from jax import lax
+from jax.experimental import pallas as pl
+from jax.experimental.pallas import tpu as pltpu
 from jax.sharding import PartitionSpec as P
 
-
-def local(tokens, active, placement_map, enc_weight, enc_bias, dec_weight, dec_bias):
+SIXTHS = (12, 12)
+ORDER = (
+    "named.0", "x.0", "all.0", "b1.0", "setup.0", "x.1", "wa1.0", "b2.0", "b1.1", "a1.1", "c2.0",
+    "ena.0", "c3.0", "c1.1", "b2.1", "wc2.0", "c2.1", "dea.0", "wc3.0", "s1.0", "enb.0", "wb2.1",
+    "wc1.1", "c3.1", "ena.1", "ws1.0", "wc2.1", "deb.0", "s3.0", "s2.0", "dea.1", "wc3.1", "s1.1",
+    "enb.1", "t2.0", "t1.0", "deb.1", "s3.1", "wt2.0", "ws1.1", "u1.0", "s2.1", "wt1.0", "t2.1",
+    "fin.0", "t1.1", "u1.1", "wt1.1", "fin.1",
+)
+TO_MID = [(0, 1), (3, 2)]
+ACROSS = [(1, 2), (2, 1)]
+TO_END = [(1, 0), (2, 3)]
+SWAP = [(0, 1), (1, 0)]
+BF = jnp.bfloat16
+F32 = jnp.float32
+WSPEC = pl.BlockSpec(memory_space=pltpu.VMEM)
+VMEM = 20 << 20
+DTILE = 1024
+ONEAR = True
+
+
+def encode_kernel(slots, off, s_ref, pos, *refs):
+    half = len(slots)
+    at_end, at_mid = refs[:half], refs[half:2 * half]
+    wo, wp, out, xs, pre, sem = refs[2 * half:]
+    r = out.shape[0] // half
+    top = pos.shape[2]
+    bw = out.shape[1] // top
+    cols = wo.shape[1]
+    end = s_ref[0] == 1
+
+    def move(i, src):
+        return pltpu.make_async_copy(src, xs.at[i * r:(i + 1) * r], sem.at[i])
+
+    @pl.when(end)
+    def _():
+        for i, src in enumerate(at_end):
+            move(i, src).start()
+
+    @pl.when(jnp.logical_not(end))
+    def _():
+        for i, src in enumerate(at_mid):
+            move(i, src).start()
+
+    for i in range(half):
+        move(i, at_end[i]).wait()
+    pre[:, :cols] = jnp.dot(xs[...], wo[...], preferred_element_type=F32)
+    pre[:, cols:] = jnp.dot(xs[...], wp[...], preferred_element_type=F32)
+    step = next(n for n in (64, 48, 32, 16) if r % n == 0)
+    for i, slot in enumerate(slots):
+        for at in range(0, r, step):
+            p = pos[s_ref[3 + slot], off + at:off + at + step, :]
+            rs = slice(i * r + at, i * r + at + step)
+            for k in range(top):
+                q = jnp.broadcast_to(p[:, k:k + 1], (step, bw))
+                a = jnp.zeros((step, bw), F32)
+                for b in range(2 * cols // bw):
+                    base = s_ref[1] + b if b < cols // bw else s_ref[2] + b - cols // bw
+                    a = jnp.where(q == base, pre[rs, b * bw:(b + 1) * bw], a)
+                out[rs, k * bw:(k + 1) * bw] = a.astype(BF)
+
+
+def decode_kernel(slots, off, s_ref, pos, own, px, py, pd, bo, bp, wo, wp, *refs):
+    outs, codes = refs[:-1], refs[-1]
+    top = pos.shape[2]
+    bw = own.shape[1] // top
+    r = outs[0].shape[0]
+    h, width = wo.shape
+    for i, slot in enumerate(slots):
+        p = pos[s_ref[3 + slot], off:off + r, :]
+        rs = slice(i * r, (i + 1) * r)
+        wide = [jnp.broadcast_to(p[:, k:k + 1], (r, bw)) for k in range(top)]
+        tot = [own[rs, c].astype(F32) + px[rs, c].astype(F32) + (py[rs, c].astype(F32) + pd[rs, c].astype(F32))
+               for c in (slice(k * bw, (k + 1) * bw) for k in range(top))]
+        for bias, base, at in ((bo, s_ref[1], 0), (bp, s_ref[2], h)):
+            for b in range(h // bw):
+                v = jnp.full((r, bw), -jnp.inf, F32)
+                for k in range(top):
+                    v = jnp.where(wide[k] == base + b, tot[k], v)
+                codes[rs, at + b * bw:at + (b + 1) * bw] = jnp.maximum(v + bias[:, b * bw:(b + 1) * bw], 0.0).astype(BF)
+    tile = DTILE
+    for n in range(width // tile):
+        c = slice(n * tile, (n + 1) * tile)
+        y = jnp.dot(codes[:, :h], wo[:, c], preferred_element_type=F32) + jnp.dot(
+            codes[:, h:], wp[:, c], preferred_element_type=F32)
+        for i, o in enumerate(outs):
+            o[:, c] = y[i * r:(i + 1) * r].astype(o.dtype)
+
+
+NEAR, FAR = pl.BlockSpec(memory_space=pltpu.VMEM), pl.BlockSpec(memory_space=pl.ANY)
+
+
+def encode(scal, pos, off, slots, at_end, at_mid, wo, wp, bw):
+    r, width = at_end[0].shape
+    cols = wo.shape[1]
+    top = pos.shape[2]
+    n = len(slots)
+    return pl.pallas_call(
+        lambda *refs: encode_kernel(slots, off, *refs),
+        out_shape=jax.ShapeDtypeStruct((n * r, top * bw), BF),
+        in_specs=[pl.BlockSpec(memory_space=pltpu.SMEM), NEAR] + [FAR] * (2 * n) + [WSPEC] * 2,
+        out_specs=NEAR if ONEAR else FAR,
+        scratch_shapes=[pltpu.VMEM((n * r, width), BF), pltpu.VMEM((n * r, 2 * cols), F32), pltpu.SemaphoreType.DMA((n,))],
+        compiler_params=pltpu.CompilerParams(vmem_limit_bytes=VMEM),
+        cost_estimate=pl.CostEstimate(flops=1, bytes_accessed=1, transcendentals=0),
+        name="encode",
+    )(scal, pos, *at_end, *at_mid, wo, wp)
+
+
+def decode(scal, pos, off, slots, kinds, parts, bo, bp, wo, wp):
+    n = len(slots)
+    r = parts[0].shape[0] // n
+    half, width = wo.shape
+    return pl.pallas_call(
+        lambda *refs: decode_kernel(slots, off, *refs),
+        out_shape=[jax.ShapeDtypeStruct((r, width), kind) for kind in kinds],
+        in_specs=[pl.BlockSpec(memory_space=pltpu.SMEM)] + [NEAR] * 7 + [WSPEC] * 2,
+        out_specs=[NEAR] * n,
+        scratch_shapes=[pltpu.VMEM((n * r, 2 * half), BF)],
+        compiler_params=pltpu.CompilerParams(vmem_limit_bytes=VMEM),
+        cost_estimate=pl.CostEstimate(flops=1, bytes_accessed=1, transcendentals=0),
+        name="decode",
+    )(scal, pos, *parts, bo, bp, wo, wp)
+
+
+def line(tokens, active, placement_map, enc_weight, enc_bias, dec_weight, dec_bias):
+    rows, width = tokens.shape
+    nblocks = placement_map.shape[0]
+    nseq, nlat = lax.axis_size("seq"), lax.axis_size("lat")
+    local_blocks = nblocks // (nseq * nlat)
+    bw = enc_bias.shape[0] // local_blocks
+    s, l = lax.axis_index("seq"), lax.axis_index("lat")
+    chunks = len(SIXTHS)
+    sizes = [rows * n // sum(SIXTHS) for n in SIXTHS]
+    offs = [sum(sizes[:c]) for c in range(chunks)]
+    pp = lax.ppermute
+    f32 = lambda z: z.astype(F32)
+    last = ()
+    v = [dict() for _ in range(chunks)]
+    m = {}
+    at_end = (s == 0) | (s == nseq - 1)
+
+    def after(*vals):
+        if last:
+            vals = lax.optimization_barrier(tuple(vals) + tuple(last))[:len(vals)]
+        return vals
+
+    def mark(*vals):
+        nonlocal last
+        last = vals
+
+    def wait(d, *names):
+        vals = after(*[d[n] for n in names])
+        d.update(zip(names, vals))
+        mark(*vals)
+
+    def named():
+        ids = jnp.arange(nblocks, dtype=jnp.int32)
+        pos = jnp.sum(jnp.where(active[:, :, None] == ids, placement_map, 0), axis=2)
+        m["n0"] = pos
+        for k in range(1, nseq):
+            m[f"n{k}"] = pp(pos, "seq", [(i, (i + k) % nseq) for i in range(nseq)])
+        wait(m, *[f"n{k}" for k in range(1, nseq)])
+        m["pos"] = jnp.stack([m[f"n{k}"] for k in range(nseq)])
+
+    def setup():
+        ew, dw = after(enc_weight, dec_weight)
+        m["ep"] = pp(ew, "lat", SWAP)
+        m["dp"] = pp(dw, "lat", SWAP)
+        m["bo"] = enc_bias[None, :]
+        m["bp"] = pp(m["bo"], "lat", SWAP)
+        at = jnp.array([[0, 1, 2, 3], [1, 2, 3, 0], [2, 1, 0, 3], [3, 2, 1, 0]], jnp.int32)
+        m["scal"] = jnp.concatenate([jnp.stack([at_end.astype(jnp.int32), (s * nlat + l) * local_blocks,
+                                                (s * nlat + 1 - l) * local_blocks]), lax.rem(s - at[s] + nseq, nseq)])
+
+    def step(name, c):
+        d = v[c]
+        if name == "x":
+            (x,) = after(tokens[offs[c]:offs[c] + sizes[c]])
+            d["x"] = (f32(x) - dec_bias[None, :]).astype(BF)
+            mark(d["x"])
+        elif name == "all":
+            d["a1"] = d["c1"] = pp(after(d["x"])[0], "seq", TO_MID + TO_END)
+        elif name == "setup":
+            setup()
+        elif name == "named":
+            named()
+        elif name == "a1":
+            d["a1"] = pp(after(d["x"])[0], "seq", TO_MID)
+        elif name == "b1":
+            d["b1"] = pp(after(d["x"])[0], "seq", ACROSS)
+        elif name == "c1":
+            d["c1"] = pp(after(d["x"])[0], "seq", TO_END)
+        elif name == "b2":
+            wait(d, "a1")
+            d["b2"] = pp(d["a1"], "seq", ACROSS)
+        elif name == "c2":
+            wait(d, "b1")
+            d["c2"] = pp(d["b1"], "seq", TO_END)
+        elif name == "c3":
+            wait(d, "b2")
+            d["c3"] = pp(d["b2"], "seq", TO_END)
+        elif name in ("wxa", "wxb"):
+            wait(d, *["p" + name[2] + n for n in ("d", "x", "y")])
+        elif name[0] == "w":
+            wait(d, name[1:])
+        elif name in ("ena", "enb"):
+            h = name[2]
+            ends, mids, slots = (("x", "c1"), ("x", "b1"), (0, 1)) if h == "a" else (("c2", "c3"), ("b2", "a1"), (2, 3))
+            rows = after(*[d[n] for n in ends + mids])
+            pb = encode(m["scal"], m["pos"], offs[c], slots, rows[:2], rows[2:], enc_weight, m["ep"], bw)
+            mark(pb)
+            d["p" + h] = pb
+            for n, p in (("d", [(0, 3), (3, 0), (1, 2), (2, 1)]), ("x", [(0, 1), (1, 0), (2, 3), (3, 2)]),
+                         ("y", [(0, 2), (2, 0), (1, 3), (3, 1)])):
+                d["p" + h + n] = pp(pb, "tp", p)
+        elif name in ("dea", "deb"):
+            h = name[2]
+            parts = after(*[d["p" + h + n] for n in ("", "x", "y", "d")])
+            slots, kinds, ys = ((0, 1), (F32, BF), ("y0", "y1")) if h == "a" else ((2, 3), (BF, BF), ("y2", "y3"))
+            out = decode(m["scal"], m["pos"], offs[c], slots, kinds, parts, m["bo"], m["bp"], dec_weight, m["dp"])
+            mark(*out)
+            d.update(zip(ys, out))
+        elif name in ("s3", "s2", "s1"):
+            d[name] = pp(after(d["y" + name[1]])[0], "seq", TO_MID)
+        elif name in ("t2", "t1"):
+            wait(d, "s3" if name == "t2" else "s2")
+            z = (f32(d["y" + name[1]]) + f32(d["s3" if name == "t2" else "s2"])).astype(BF)
+            mark(z)
+            d[name] = pp(z, "seq", ACROSS)
+        elif name == "u1":
+            wait(d, "t2")
+            z = (f32(d["y3"]) + f32(d["t2"])).astype(BF)
+            mark(z)
+            d[name] = pp(z, "seq", TO_END)
+        elif name == "fin":
+            wait(d, "s1", "t1", "u1")
+            d["out"] = (d["y0"] + (f32(d["s1"]) + f32(d["t1"]) + f32(d["u1"])) + dec_bias[None, :]).astype(BF)
+            mark(d["out"])
+        else:
+            raise ValueError(name)
+
+    for item in ORDER:
+        name, c = item.split(".")
+        step(name, int(c))
+    return jnp.concatenate([d["out"] for d in v])
+
+
+def general(tokens, active, placement_map, enc_weight, enc_bias, dec_weight, dec_bias):
     rows, width = tokens.shape
     top = active.shape[1]
     nblocks = placement_map.shape[0]
@@ -53,7 +301,7 @@
 
 def solution(mesh):
     return jax.shard_map(
-        local,
+        line if dict(mesh.shape) == {"seq": 4, "tp": 4, "lat": 2} else general,
         mesh=mesh,
         in_specs=(
             P(("seq", "lat"), "tp"),

time: 621 us -> 229 us (0.37)
  waiting for transfers between devices: 462 us -> 112 us
  local copies, waits for them, and re-layouts: 81.3 us -> 7.68 us
  starting transfers between devices: 11.6 us -> 70.9 us
  Pallas kernels: 0 us -> 30.7 us
  other arithmetic: 36.6 us -> 6.7 us
  matrix products: 14.3 us -> 0 us
  between operations: 13.5 us -> 0.53 us
    all_to_all x2 -> x0, waiting for transfers between devices: 409 us -> none  [the longest x1 206 us: local(): lax.all_to_all(jnp.einsum('sbch,bhd->sbcd', codes, dec_blocks, preferred_...]
    ppermute x0 -> x41, waiting for transfers between devices: none -> 112 us  [the longest x12 37.6 us: step(): d['p' + h + n] = pp(pb, 'tp', p)]
    ppermute x0 -> x41, starting transfers between devices: none -> 70.9 us  [the longest x6 22.4 us: step(): d[name] = pp(after(d['y' + name[1]])[0], 'seq', TO_MID)]
    psum x1 -> x0, waiting for transfers between devices: 53.5 us -> none  [local(): summed = lax.psum(preact, 'tp')]
    gather x2 -> x0, local copies, waits for them, and re-layouts: 37.6 us -> none  [the longest x1 20 us: local(): centered[slot_row]]
    pallas_call x0 -> x8, Pallas kernels: none -> 30.7 us  [the longest x4 16.5 us: decode(): pl.pallas_call(lambda *refs: decode_kernel(slots, off, *refs), out_shape=...]
    convert_element_type x2 -> x0, local copies, waits for them, and re-layouts: 21.1 us -> none  [the longest x1 11.9 us: local(): contrib = returned[target].reshape(rows, top, width).astype(jnp.float32)]
    scatter x2 -> x0, local copies, waits for them, and re-layouts: 17.4 us -> none  [the longest x1 11.2 us: local(): filled = jnp.zeros((nblocks * capacity,), jnp.bool_).at[target].set(True)]
  transfers between devices with their start and end apart: 3 -> 41, of which waited for: 3 -> 19; matrix products, arithmetic and copies ran while one was open for 1% -> 3% of each run, Pallas kernels for 0% -> 13%
where the time goes in v1:
time: 229 us; the launch traced here: 228 us
  waiting for transfers between devices  112 us (49%)
  starting transfers between devices  70.9 us (31%)
  Pallas kernels  30.7 us (13%)
  local copies, waits for them, and re-layouts  7.68 us (3%)
  other arithmetic  6.7 us (3%)
    ppermute x12, waiting for transfers between devices, step(): d['p' + h + n] = pp(pb, 'tp', p)  37.6 us
    ppermute x6, waiting for transfers between devices, step(): d[name] = pp(after(d['y' + name[1]])[0], 'seq', TO_MID)  24.3 us
    ppermute x6, starting transfers between devices, step(): d[name] = pp(after(d['y' + name[1]])[0], 'seq', TO_MID)  22.4 us
    ppermute x12, starting transfers between devices, step(): d['p' + h + n] = pp(pb, 'tp', p)  17.8 us
    ppermute x2, waiting for transfers between devices, step(): d[name] = pp(z, 'seq', TO_END)  17.3 us
    ppermute x1, waiting for transfers between devices, step(): d['a1'] = d['c1'] = pp(after(d['x'])[0], 'seq', TO_MID + TO_END)  16.9 us
    pallas_call x4, Pallas kernels, decode(): pl.pallas_call(lambda *refs: decode_kernel(slots, off, *refs), out_shape=...  16.5 us
    pallas_call x4, Pallas kernels, encode(): pl.pallas_call(lambda *refs: encode_kernel(slots, off, *refs), out_shape=...  14.2 us
  transfers between devices with their start and end apart: 41, of which 19 were waited for; matrix products, arithmetic and copies ran while one was open for 3% of the time, Pallas kernels for 13%

profile of v1, /device:TPU:0, one launch (start us, length us, event | category | flops | bytes accessed | tf_op | source)
XLA Modules:
  0.0 228.1 jit_solution(15046103191839511561)
XLA Ops:
  0.8 3.1 %collective-permute-start = (s32[384,4]{0,1:T(4,128)S(1)}, s32[384,4]{0,1:T(4,128)S(1)}, u32[]{:S(2)}, u32[]{:S(2)}) collective-permute-start(s32[384,4]{0,1:T(4,128)S(1)} %select_reduce_fusion), channel_id=1, source_target_pairs={{0,8},{8,16},{16,24},{24,0},{1,9},{9,17},{17,25},{25,1},{2,10},{10... | collective-permute-start | bytes 18440 | tf_op jit(solution)/shard_map/ppermute | solution.py:168
  3.9 2.6 %collective-permute-start.1 = (s32[384,4]{0,1:T(4,128)S(1)}, s32[384,4]{0,1:T(4,128)S(1)}, u32[]{:S(2)}, u32[]{:S(2)}) collective-permute-start(s32[384,4]{0,1:T(4,128)S(1)} %select_reduce_fusion), channel_id=1, source_target_pairs={{0,16},{8,24},{16,0},{24,8},{1,17},{9,25},{17,1},{25,9},{2,18},{10... | collective-permute-start | bytes 18440 | tf_op jit(solution)/shard_map/ppermute | solution.py:168
  7.8 1.7 fusion.1
  10.6 1.6 collective-permute-start.4
  13.6 16.9 %collective-permute-done.3.refs_3_.refs_5_ = bf16[192,2048]{1,0:T(8,128)(2,1)} collective-permute-done((bf16[192,2048]{1,0:T(8,128)(2,1)S(1)}, bf16[192,2048]{1,0:T(8,128)(2,1)}, u32[]{:S(2)}, u32[]{:S(2)}) %collective-permute-start.3) | collective-permute-done | bytes 786464 | tf_op jit(solution)/shard_map/ppermute | solution.py:189
  32.0 5.7 %collective-permute-start.11 = (bf16[192,2048]{1,0:T(8,128)(2,1)}, bf16[192,2048]{1,0:T(8,128)(2,1)}, u32[]{:S(2)}, u32[]{:S(2)}) collective-permute-start(bf16[192,2048]{1,0:T(8,128)(2,1)} %subtract_convert_fusion.refs_2_.refs_4_), channel_id=1, source_target_pairs={{0,8},{24,16},{1,9},{25,17},{2,10},{26,18},{3,11},{27,19},{4,12},{... | collective-permute-start | bytes 2359304 | tf_op jit(solution)/shard_map/ppermute | solution.py:195
  44.6 1.6 copy-done.5
  47.3 3.9 %encode.4.refs_2_ = bf16[384,512]{1,0:T(8,128)(2,1)S(1)} custom-call(s32[7]{0:T(128)S(1)} %pad_add_fusion.1.refs_0_, s32[4,384,4]{2,1,0:T(8,128)S(1)} %copy.20.refs_1_, bf16[192,2048]{1,0:T(8,128)(2,1)S(1)} %copy-done.8, bf16[192,2048]{1,0:T(8,128)(2,1)} %collective-permute-done.3.refs_3_.refs_5_, bf16[192,2048]{1,0:T(8,128)(2,1)S(1)} %copy-done.8, ...), custom_call_target="tpu_custom_call" | custom-call | flops 1 | bytes 1 | tf_op jit(solution)/shard_map/encode/pallas_call | solution.py:104
  55.1 5.3 %collective-permute-done.10.refs_2_ = bf16[192,2048]{1,0:T(8,128)(2,1)} collective-permute-done((bf16[192,2048]{1,0:T(8,128)(2,1)}, bf16[192,2048]{1,0:T(8,128)(2,1)}, u32[]{:S(2)}, u32[]{:S(2)}) %collective-permute-start.10) | collective-permute-done | bytes 786464 | tf_op jit(solution)/shard_map/ppermute | solution.py:205
  63.3 2.4 %collective-permute-done.6.refs_3_ = bf16[384,512]{1,0:T(8,128)(2,1)S(1)} collective-permute-done((bf16[384,512]{1,0:T(8,128)(2,1)S(1)}, bf16[384,512]{1,0:T(8,128)(2,1)S(1)}, u32[]{:S(2)}, u32[]{:S(2)}) %collective-permute-start.6) | collective-permute-done | bytes 393248 | tf_op jit(solution)/shard_map/ppermute | solution.py:222
  66.4 10.1 %collective-permute-done.7.refs_4_ = bf16[384,512]{1,0:T(8,128)(2,1)S(1)} collective-permute-done((bf16[384,512]{1,0:T(8,128)(2,1)S(1)}, bf16[384,512]{1,0:T(8,128)(2,1)S(1)}, u32[]{:S(2)}, u32[]{:S(2)}) %collective-permute-start.7) | collective-permute-done | bytes 393248 | tf_op jit(solution)/shard_map/ppermute | solution.py:222
  79.0 4.1 %decode.4 = (f32[192,2048]{1,0:T(8,128)S(1)}, bf16[192,2048]{1,0:T(8,128)(2,1)S(1)}) custom-call(s32[7]{0:T(128)S(1)} %pad_add_fusion.1.refs_0_, s32[4,384,4]{2,1,0:T(8,128)S(1)} %copy.20.refs_1_, bf16[384,512]{1,0:T(8,128)(2,1)S(1)} %encode.4.refs_2_, bf16[384,512]{1,0:T(8,128)(2,1)S(1)} %collective-permute-done.6.refs_3_, ...), custom_call_target="tpu_custom_call" | custom-call | flops 1 | bytes 1 | tf_op jit(solution)/shard_map/decode/pallas_call | solution.py:120
  83.2 5.0 %collective-permute-start.16 = (bf16[192,2048]{1,0:T(8,128)(2,1)S(1)}, bf16[192,2048]{1,0:T(8,128)(2,1)S(1)}, u32[]{:S(2)}, u32[]{:S(2)}) collective-permute-start(bf16[192,2048]{1,0:T(8,128)(2,1)S(1)} %get-tuple-element.110), channel_id=1, source_target_pairs={{0,8},{24,16},{1,9},{25,17},{2,10},{26,18},{3,11},{27,19},{4,12},{... | collective-permute-start | bytes 2359304 | tf_op jit(solution)/shard_map/ppermute | solution.py:231
  89.5 3.8 %encode.5.refs_2_ = bf16[384,512]{1,0:T(8,128)(2,1)S(1)} custom-call(s32[7]{0:T(128)S(1)} %pad_add_fusion.1.refs_0_, s32[4,384,4]{2,1,0:T(8,128)S(1)} %copy.20.refs_1_, bf16[192,2048]{1,0:T(8,128)(2,1)} %collective-permute-done.10.refs_2_, bf16[192,2048]{1,0:T(8,128)(2,1)S(1)} %collective-permute-done.15.refs_3_, ...), custom_call_target="tpu_custom_call" | custom-call | flops 1 | bytes 1 | tf_op jit(solution)/shard_map/encode/pallas_call | solution.py:104
  96.7 3.5 %collective-permute-start.21 = (bf16[384,512]{1,0:T(8,128)(2,1)S(1)}, bf16[384,512]{1,0:T(8,128)(2,1)S(1)}, u32[]{:S(2)}, u32[]{:S(2)}) collective-permute-start(bf16[384,512]{1,0:T(8,128)(2,1)S(1)} %encode.5.refs_2_), channel_id=1, source_target_pairs={{0,6},{6,0},{2,4},{4,2},{1,7},{7,1},{3,5},{5,3},{8,14},{14,8},{10,... | collective-permute-start | bytes 1179656 | tf_op jit(solution)/shard_map/ppermute | solution.py:222
  100.2 3.8 %encode.6.refs_2_ = bf16[384,512]{1,0:T(8,128)(2,1)S(1)} custom-call(s32[7]{0:T(128)S(1)} %pad_add_fusion.1.refs_0_, s32[4,384,4]{2,1,0:T(8,128)S(1)} %copy.20.refs_1_, bf16[192,2048]{1,0:T(8,128)(2,1)} %subtract_convert_fusion.refs_2_.refs_4_, bf16[192,2048]{1,0:T(8,128)(2,1)S(1)} %collective-permute-done.17.refs_3_, ...), custom_call_target="tpu_custom_call" | custom-call | flops 1 | bytes 1 | tf_op jit(solution)/shard_map/encode/pallas_call | solution.py:104
  106.4 7.1 %collective-permute-done.22.refs_2_ = bf16[192,2048]{1,0:T(8,128)(2,1)S(1)} collective-permute-done((bf16[192,2048]{1,0:T(8,128)(2,1)}, bf16[192,2048]{1,0:T(8,128)(2,1)S(1)}, u32[]{:S(2)}, u32[]{:S(2)}) %collective-permute-start.22) | collective-permute-done | bytes 786464 | tf_op jit(solution)/shard_map/ppermute | solution.py:205
  113.8 4.1 %decode.5 = (bf16[192,2048]{1,0:T(8,128)(2,1)S(1)}, bf16[192,2048]{1,0:T(8,128)(2,1)S(1)}) custom-call(s32[7]{0:T(128)S(1)} %pad_add_fusion.1.refs_0_, s32[4,384,4]{2,1,0:T(8,128)S(1)} %copy.20.refs_1_, bf16[384,512]{1,0:T(8,128)(2,1)S(1)} %encode.5.refs_2_, bf16[384,512]{1,0:T(8,128)(2,1)S(1)} %collective-permute-done.19.refs_3_, ...), custom_call_target="tpu_custom_call" | custom-call | flops 1 | bytes 1 | tf_op jit(solution)/shard_map/decode/pallas_call | solution.py:120
  118.0 4.6 %collective-permute-start.24 = (bf16[192,2048]{1,0:T(8,128)(2,1)S(1)}, bf16[192,2048]{1,0:T(8,128)(2,1)S(1)}, u32[]{:S(2)}, u32[]{:S(2)}) collective-permute-start(bf16[192,2048]{1,0:T(8,128)(2,1)S(1)} %get-tuple-element.132), channel_id=1, source_target_pairs={{0,8},{24,16},{1,9},{25,17},{2,10},{26,18},{3,11},{27,19},{4,12},{... | collective-permute-start | bytes 2359304 | tf_op jit(solution)/shard_map/ppermute | solution.py:231
  126.1 8.6 %collective-permute-done.26.refs_3_ = bf16[384,512]{1,0:T(8,128)(2,1)S(1)} collective-permute-done((bf16[384,512]{1,0:T(8,128)(2,1)S(1)}, bf16[384,512]{1,0:T(8,128)(2,1)S(1)}, u32[]{:S(2)}, u32[]{:S(2)}) %collective-permute-start.26) | collective-permute-done | bytes 393248 | tf_op jit(solution)/shard_map/ppermute | solution.py:222
  136.2 5.2 %collective-permute-done.27.refs_4_ = bf16[384,512]{1,0:T(8,128)(2,1)S(1)} collective-permute-done((bf16[384,512]{1,0:T(8,128)(2,1)S(1)}, bf16[384,512]{1,0:T(8,128)(2,1)S(1)}, u32[]{:S(2)}, u32[]{:S(2)}) %collective-permute-start.27) | collective-permute-done | bytes 393248 | tf_op jit(solution)/shard_map/ppermute | solution.py:222
  141.4 4.1 %decode.6 = (f32[192,2048]{1,0:T(8,128)S(1)}, bf16[192,2048]{1,0:T(8,128)(2,1)S(1)}) custom-call(s32[7]{0:T(128)S(1)} %pad_add_fusion.1.refs_0_, s32[4,384,4]{2,1,0:T(8,128)S(1)} %copy.20.refs_1_, bf16[384,512]{1,0:T(8,128)(2,1)S(1)} %encode.6.refs_2_, bf16[384,512]{1,0:T(8,128)(2,1)S(1)} %collective-permute-done.26.refs_3_, ...), custom_call_target="tpu_custom_call" | custom-call | flops 1 | bytes 1 | tf_op jit(solution)/shard_map/decode/pallas_call | solution.py:120
  145.5 2.8 %encode.7.refs_2_ = bf16[384,512]{1,0:T(8,128)(2,1)S(1)} custom-call(s32[7]{0:T(128)S(1)} %pad_add_fusion.1.refs_0_, s32[4,384,4]{2,1,0:T(8,128)S(1)} %copy.20.refs_1_, bf16[192,2048]{1,0:T(8,128)(2,1)S(1)} %collective-permute-done.22.refs_2_, bf16[192,2048]{1,0:T(8,128)(2,1)S(1)} %collective-permute-done.25.refs_3_, ...), custom_call_target="tpu_custom_call" | custom-call | flops 1 | bytes 1 | tf_op jit(solution)/shard_map/encode/pallas_call | solution.py:104
  149.3 5.2 %collective-permute-start.34 = (bf16[192,2048]{1,0:T(8,128)(2,1)S(1)}, bf16[192,2048]{1,0:T(8,128)(2,1)S(1)}, u32[]{:S(2)}, u32[]{:S(2)}) collective-permute-start(bf16[192,2048]{1,0:T(8,128)(2,1)S(1)} %get-tuple-element.153), channel_id=1, source_target_pairs={{0,8},{24,16},{1,9},{25,17},{2,10},{26,18},{3,11},{27,19},{4,12},{... | collective-permute-start | bytes 2359304 | tf_op jit(solution)/shard_map/ppermute | solution.py:231
  159.1 6.2 %collective-permute-done.31.refs_3_ = bf16[384,512]{1,0:T(8,128)(2,1)S(1)} collective-permute-done((bf16[384,512]{1,0:T(8,128)(2,1)S(1)}, bf16[384,512]{1,0:T(8,128)(2,1)S(1)}, u32[]{:S(2)}, u32[]{:S(2)}) %collective-permute-start.31) | collective-permute-done | bytes 393248 | tf_op jit(solution)/shard_map/ppermute | solution.py:222
  166.0 5.0 %collective-permute-done.32.refs_4_ = bf16[384,512]{1,0:T(8,128)(2,1)S(1)} collective-permute-done((bf16[384,512]{1,0:T(8,128)(2,1)S(1)}, bf16[384,512]{1,0:T(8,128)(2,1)S(1)}, u32[]{:S(2)}, u32[]{:S(2)}) %collective-permute-start.32) | collective-permute-done | bytes 393248 | tf_op jit(solution)/shard_map/ppermute | solution.py:222
  171.0 4.1 %decode.7 = (bf16[192,2048]{1,0:T(8,128)(2,1)S(1)}, bf16[192,2048]{1,0:T(8,128)(2,1)S(1)}) custom-call(s32[7]{0:T(128)S(1)} %pad_add_fusion.1.refs_0_, s32[4,384,4]{2,1,0:T(8,128)S(1)} %copy.20.refs_1_, bf16[384,512]{1,0:T(8,128)(2,1)S(1)} %encode.7.refs_2_, bf16[384,512]{1,0:T(8,128)(2,1)S(1)} %collective-permute-done.31.refs_3_, ...), custom_call_target="tpu_custom_call" | custom-call | flops 1 | bytes 1 | tf_op jit(solution)/shard_map/decode/pallas_call | solution.py:120
  175.1 1.7 collective-permute-start.36
  178.4 11.7 %collective-permute-done.36 = bf16[192,2048]{1,0:T(8,128)(2,1)S(1)} collective-permute-done((bf16[192,2048]{1,0:T(8,128)(2,1)S(1)}, bf16[192,2048]{1,0:T(8,128)(2,1)S(1)}, u32[]{:S(2)}, u32[]{:S(2)}) %collective-permute-start.36) | collective-permute-done | bytes 786464 | tf_op jit(solution)/shard_map/ppermute | solution.py:231
  190.1 4.4 %collective-permute-start.37 = (bf16[192,2048]{1,0:T(8,128)(2,1)S(1)}, bf16[192,2048]{1,0:T(8,128)(2,1)S(1)}, u32[]{:S(2)}, u32[]{:S(2)}) collective-permute-start(bf16[192,2048]{1,0:T(8,128)(2,1)S(1)} %get-tuple-element.162), channel_id=1, source_target_pairs={{0,8},{24,16},{1,9},{25,17},{2,10},{26,18},{3,11},{27,19},{4,12},{... | collective-permute-start | bytes 2359304 | tf_op jit(solution)/shard_map/ppermute | solution.py:231
  196.0 10.4 %collective-permute-done.37 = bf16[192,2048]{1,0:T(8,128)(2,1)S(1)} collective-permute-done((bf16[192,2048]{1,0:T(8,128)(2,1)S(1)}, bf16[192,2048]{1,0:T(8,128)(2,1)S(1)}, u32[]{:S(2)}, u32[]{:S(2)}) %collective-permute-start.37) | collective-permute-done | bytes 786464 | tf_op jit(solution)/shard_map/ppermute | solution.py:231
  209.1 17.3 %collective-permute-done.40 = bf16[192,2048]{1,0:T(8,128)(2,1)S(1)} collective-permute-done((bf16[192,2048]{1,0:T(8,128)(2,1)S(1)}, bf16[192,2048]{1,0:T(8,128)(2,1)S(1)}, u32[]{:S(2)}, u32[]{:S(2)}) %collective-permute-start.40) | collective-permute-done | bytes 786464 | tf_op jit(solution)/shard_map/ppermute | solution.py:241
  (97 shorter events, 50.3 us)
Async XLA Ops:
  10.3 28.7 %collective-permute-start.5 = (bf16[2048,512]{1,0:T(8,128)(2,1)S(1)}, bf16[2048,512]{1,0:T(8,128)(2,1)S(1)}, u32[]{:S(2)}, u32[]{:S(2)}) collective-permute-start(bf16[2048,512]{1,0:T(8,128)(2,1)S(1)} %copy-done.1), channel_id=1, source_target_pairs={{0,1},{1,0},{2,3},{3,2},{4,5},{5,4},{6,7},{7,6},{8,9},{9,8},{10,11... | collective-permute-start | bytes 6291464 | tf_op jit(solution)/shard_map/ppermute | solution.py:174
  10.4 20.1 %collective-permute-start.3 = (bf16[192,2048]{1,0:T(8,128)(2,1)S(1)}, bf16[192,2048]{1,0:T(8,128)(2,1)}, u32[]{:S(2)}, u32[]{:S(2)}) collective-permute-start(bf16[192,2048]{1,0:T(8,128)(2,1)S(1)} %subtract_convert_fusion.1.refs_2_.refs_4_), channel_id=1, source_target_pairs={{0,8},{24,16},{8,0},{16,24},{1,9},{25,17},{9,1},{17,25},{2,10},{26... | collective-permute-start | bytes 2359304 | tf_op jit(solution)/shard_map/ppermute | solution.py:189
  10.6 27.1 %collective-permute-start.4 = (bf16[192,2048]{1,0:T(8,128)(2,1)S(1)}, bf16[192,2048]{1,0:T(8,128)(2,1)}, u32[]{:S(2)}, u32[]{:S(2)}) collective-permute-start(bf16[192,2048]{1,0:T(8,128)(2,1)S(1)} %subtract_convert_fusion.1.refs_2_.refs_4_), channel_id=1, source_target_pairs={{8,16},{16,8},{9,17},{17,9},{10,18},{18,10},{11,19},{19,11},{12,20... | collective-permute-start | bytes 2359304 | tf_op jit(solution)/shard_map/ppermute | solution.py:197
  12.2 66.8 %collective-permute-start.14 = (bf16[512,2048]{1,0:T(8,128)(2,1)S(1)}, bf16[512,2048]{1,0:T(8,128)(2,1)}, u32[]{:S(2)}, u32[]{:S(2)}) collective-permute-start(bf16[512,2048]{1,0:T(8,128)(2,1)S(1)} %copy-done), channel_id=1, source_target_pairs={{0,1},{1,0},{2,3},{3,2},{4,5},{5,4},{6,7},{7,6},{8,9},{9,8},{10,11... | collective-permute-start | bytes 6291464 | tf_op jit(solution)/shard_map/ppermute | solution.py:175
  30.5 20.7 %collective-permute-start.12 = (bf16[192,2048]{1,0:T(8,128)(2,1)}, bf16[192,2048]{1,0:T(8,128)(2,1)}, u32[]{:S(2)}, u32[]{:S(2)}) collective-permute-start(bf16[192,2048]{1,0:T(8,128)(2,1)} %collective-permute-done.3.refs_3_.refs_5_), channel_id=1, source_target_pairs={{8,16},{16,8},{9,17},{17,9},{10,18},{18,10},{11,19},{19,11},{12,20... | collective-permute-start | bytes 2359304 | tf_op jit(solution)/shard_map/ppermute | solution.py:202
  32.0 21.6 %collective-permute-start.11 = (bf16[192,2048]{1,0:T(8,128)(2,1)}, bf16[192,2048]{1,0:T(8,128)(2,1)}, u32[]{:S(2)}, u32[]{:S(2)}) collective-permute-start(bf16[192,2048]{1,0:T(8,128)(2,1)} %subtract_convert_fusion.refs_2_.refs_4_), channel_id=1, source_target_pairs={{0,8},{24,16},{1,9},{25,17},{2,10},{26,18},{3,11},{27,19},{4,12},{... | collective-permute-start | bytes 2359304 | tf_op jit(solution)/shard_map/ppermute | solution.py:195
  37.7 22.7 %collective-permute-start.10 = (bf16[192,2048]{1,0:T(8,128)(2,1)}, bf16[192,2048]{1,0:T(8,128)(2,1)}, u32[]{:S(2)}, u32[]{:S(2)}) collective-permute-start(bf16[192,2048]{1,0:T(8,128)(2,1)} %collective-permute-done.4.refs_5_), channel_id=1, source_target_pairs={{8,0},{16,24},{9,1},{17,25},{10,2},{18,26},{11,3},{19,27},{12,4},{... | collective-permute-start | bytes 2359304 | tf_op jit(solution)/shard_map/ppermute | solution.py:205
  40.4 21.5 %collective-permute-start.9 = (bf16[192,2048]{1,0:T(8,128)(2,1)}, bf16[192,2048]{1,0:T(8,128)(2,1)}, u32[]{:S(2)}, u32[]{:S(2)}) collective-permute-start(bf16[192,2048]{1,0:T(8,128)(2,1)} %subtract_convert_fusion.refs_2_.refs_4_), channel_id=1, source_target_pairs={{8,16},{16,8},{9,17},{17,9},{10,18},{18,10},{11,19},{19,11},{12,20... | collective-permute-start | bytes 2359304 | tf_op jit(solution)/shard_map/ppermute | solution.py:197
  51.2 32.0 %collective-permute-start.15 = (bf16[192,2048]{1,0:T(8,128)(2,1)}, bf16[192,2048]{1,0:T(8,128)(2,1)S(1)}, u32[]{:S(2)}, u32[]{:S(2)}) collective-permute-start(bf16[192,2048]{1,0:T(8,128)(2,1)} %collective-permute-done.12.refs_4_), channel_id=1, source_target_pairs={{8,0},{16,24},{9,1},{17,25},{10,2},{18,26},{11,3},{19,27},{12,4},{... | collective-permute-start | bytes 2359304 | tf_op jit(solution)/shard_map/ppermute | solution.py:208
  60.4 16.1 %collective-permute-start.7 = (bf16[384,512]{1,0:T(8,128)(2,1)S(1)}, bf16[384,512]{1,0:T(8,128)(2,1)S(1)}, u32[]{:S(2)}, u32[]{:S(2)}) collective-permute-start(bf16[384,512]{1,0:T(8,128)(2,1)S(1)} %encode.4.refs_2_), channel_id=1, source_target_pairs={{0,4},{4,0},{2,6},{6,2},{1,5},{5,1},{3,7},{7,3},{8,12},{12,8},{10,... | collective-permute-start | bytes 1179656 | tf_op jit(solution)/shard_map/ppermute | solution.py:222
  61.9 15.8 %collective-permute-start.8 = (bf16[384,512]{1,0:T(8,128)(2,1)S(1)}, bf16[384,512]{1,0:T(8,128)(2,1)S(1)}, u32[]{:S(2)}, u32[]{:S(2)}) collective-permute-start(bf16[384,512]{1,0:T(8,128)(2,1)S(1)} %encode.4.refs_2_), channel_id=1, source_target_pairs={{0,6},{6,0},{2,4},{4,2},{1,7},{7,1},{3,5},{5,3},{8,14},{14,8},{10,... | collective-permute-start | bytes 1179656 | tf_op jit(solution)/shard_map/ppermute | solution.py:222
  65.7 29.2 %collective-permute-start.18 = (bf16[192,2048]{1,0:T(8,128)(2,1)}, bf16[192,2048]{1,0:T(8,128)(2,1)S(1)}, u32[]{:S(2)}, u32[]{:S(2)}) collective-permute-start(bf16[192,2048]{1,0:T(8,128)(2,1)} %collective-permute-done.11.refs_5_), channel_id=1, source_target_pairs={{8,16},{16,8},{9,17},{17,9},{10,18},{18,10},{11,19},{19,11},{12,20... | collective-permute-start | bytes 2359304 | tf_op jit(solution)/shard_map/ppermute | solution.py:202
  76.5 20.2 %collective-permute-start.17 = (bf16[192,2048]{1,0:T(8,128)(2,1)}, bf16[192,2048]{1,0:T(8,128)(2,1)S(1)}, u32[]{:S(2)}, u32[]{:S(2)}) collective-permute-start(bf16[192,2048]{1,0:T(8,128)(2,1)} %subtract_convert_fusion.refs_2_.refs_4_), channel_id=1, source_target_pairs={{8,0},{16,24},{9,1},{17,25},{10,2},{18,26},{11,3},{19,27},{12,4},{... | collective-permute-start | bytes 2359304 | tf_op jit(solution)/shard_map/ppermute | solution.py:199
  83.2 22.0 %collective-permute-start.16 = (bf16[192,2048]{1,0:T(8,128)(2,1)S(1)}, bf16[192,2048]{1,0:T(8,128)(2,1)S(1)}, u32[]{:S(2)}, u32[]{:S(2)}) collective-permute-start(bf16[192,2048]{1,0:T(8,128)(2,1)S(1)} %get-tuple-element.110), channel_id=1, source_target_pairs={{0,8},{24,16},{1,9},{25,17},{2,10},{26,18},{3,11},{27,19},{4,12},{... | collective-permute-start | bytes 2359304 | tf_op jit(solution)/shard_map/ppermute | solution.py:231
  88.2 25.4 %collective-permute-start.22 = (bf16[192,2048]{1,0:T(8,128)(2,1)}, bf16[192,2048]{1,0:T(8,128)(2,1)S(1)}, u32[]{:S(2)}, u32[]{:S(2)}) collective-permute-start(bf16[192,2048]{1,0:T(8,128)(2,1)} %collective-permute-done.9.refs_5_), channel_id=1, source_target_pairs={{8,0},{16,24},{9,1},{17,25},{10,2},{18,26},{11,3},{19,27},{12,4},{... | collective-permute-start | bytes 2359304 | tf_op jit(solution)/shard_map/ppermute | solution.py:205
  93.3 20.3 %collective-permute-start.19 = (bf16[384,512]{1,0:T(8,128)(2,1)S(1)}, bf16[384,512]{1,0:T(8,128)(2,1)S(1)}, u32[]{:S(2)}, u32[]{:S(2)}) collective-permute-start(bf16[384,512]{1,0:T(8,128)(2,1)S(1)} %encode.5.refs_2_), channel_id=1, source_target_pairs={{0,2},{2,0},{4,6},{6,4},{1,3},{3,1},{5,7},{7,5},{8,10},{10,8},{12,... | collective-permute-start | bytes 1179656 | tf_op jit(solution)/shard_map/ppermute | solution.py:222
  94.9 19.0 %collective-permute-start.20 = (bf16[384,512]{1,0:T(8,128)(2,1)S(1)}, bf16[384,512]{1,0:T(8,128)(2,1)S(1)}, u32[]{:S(2)}, u32[]{:S(2)}) collective-permute-start(bf16[384,512]{1,0:T(8,128)(2,1)S(1)} %encode.5.refs_2_), channel_id=1, source_target_pairs={{0,4},{4,0},{2,6},{6,2},{1,5},{5,1},{3,7},{7,3},{8,12},{12,8},{10,... | collective-permute-start | bytes 1179656 | tf_op jit(solution)/shard_map/ppermute | solution.py:222
  96.7 17.1 %collective-permute-start.21 = (bf16[384,512]{1,0:T(8,128)(2,1)S(1)}, bf16[384,512]{1,0:T(8,128)(2,1)S(1)}, u32[]{:S(2)}, u32[]{:S(2)}) collective-permute-start(bf16[384,512]{1,0:T(8,128)(2,1)S(1)} %encode.5.refs_2_), channel_id=1, source_target_pairs={{0,6},{6,0},{2,4},{4,2},{1,7},{7,1},{3,5},{5,3},{8,14},{14,8},{10,... | collective-permute-start | bytes 1179656 | tf_op jit(solution)/shard_map/ppermute | solution.py:222
  105.1 40.3 %collective-permute-start.25 = (bf16[192,2048]{1,0:T(8,128)(2,1)S(1)}, bf16[192,2048]{1,0:T(8,128)(2,1)S(1)}, u32[]{:S(2)}, u32[]{:S(2)}) collective-permute-start(bf16[192,2048]{1,0:T(8,128)(2,1)S(1)} %collective-permute-done.18.refs_4_), channel_id=1, source_target_pairs={{8,0},{16,24},{9,1},{17,25},{10,2},{18,26},{11,3},{19,27},{12,4},{... | collective-permute-start | bytes 2359304 | tf_op jit(solution)/shard_map/ppermute | solution.py:208
  118.0 30.3 %collective-permute-start.24 = (bf16[192,2048]{1,0:T(8,128)(2,1)S(1)}, bf16[192,2048]{1,0:T(8,128)(2,1)S(1)}, u32[]{:S(2)}, u32[]{:S(2)}) collective-permute-start(bf16[192,2048]{1,0:T(8,128)(2,1)S(1)} %get-tuple-element.132), channel_id=1, source_target_pairs={{0,8},{24,16},{1,9},{25,17},{2,10},{26,18},{3,11},{27,19},{4,12},{... | collective-permute-start | bytes 2359304 | tf_op jit(solution)/shard_map/ppermute | solution.py:231
  123.9 17.5 %collective-permute-start.27 = (bf16[384,512]{1,0:T(8,128)(2,1)S(1)}, bf16[384,512]{1,0:T(8,128)(2,1)S(1)}, u32[]{:S(2)}, u32[]{:S(2)}) collective-permute-start(bf16[384,512]{1,0:T(8,128)(2,1)S(1)} %encode.6.refs_2_), channel_id=1, source_target_pairs={{0,4},{4,0},{2,6},{6,2},{1,5},{5,1},{3,7},{7,3},{8,12},{12,8},{10,... | collective-permute-start | bytes 1179656 | tf_op jit(solution)/shard_map/ppermute | solution.py:222
  124.7 16.7 %collective-permute-start.28 = (bf16[384,512]{1,0:T(8,128)(2,1)S(1)}, bf16[384,512]{1,0:T(8,128)(2,1)S(1)}, u32[]{:S(2)}, u32[]{:S(2)}) collective-permute-start(bf16[384,512]{1,0:T(8,128)(2,1)S(1)} %encode.6.refs_2_), channel_id=1, source_target_pairs={{0,6},{6,0},{2,4},{4,2},{1,7},{7,1},{3,5},{5,3},{8,14},{14,8},{10,... | collective-permute-start | bytes 1179656 | tf_op jit(solution)/shard_map/ppermute | solution.py:222
  134.7 22.7 %collective-permute-start.23 = (bf16[192,2048]{1,0:T(8,128)(2,1)S(1)}, bf16[192,2048]{1,0:T(8,128)(2,1)S(1)}, u32[]{:S(2)}, u32[]{:S(2)}) collective-permute-start(bf16[192,2048]{1,0:T(8,128)(2,1)S(1)} %get-tuple-element.131), channel_id=1, source_target_pairs={{0,8},{24,16},{1,9},{25,17},{2,10},{26,18},{3,11},{27,19},{4,12},{... | collective-permute-start | bytes 2359304 | tf_op jit(solution)/shard_map/ppermute | solution.py:231
  148.6 28.3 %collective-permute-start.30 = (bf16[192,2048]{1,0:T(8,128)(2,1)S(1)}, bf16[192,2048]{1,0:T(8,128)(2,1)S(1)}, u32[]{:S(2)}, u32[]{:S(2)}) collective-permute-start(bf16[192,2048]{1,0:T(8,128)(2,1)S(1)} %add_convert_fusion.7), channel_id=1, source_target_pairs={{8,16},{16,8},{9,17},{17,9},{10,18},{18,10},{11,19},{19,11},{12,20... | collective-permute-start | bytes 2359304 | tf_op jit(solution)/shard_map/ppermute | solution.py:236
  149.3 27.6 %collective-permute-start.34 = (bf16[192,2048]{1,0:T(8,128)(2,1)S(1)}, bf16[192,2048]{1,0:T(8,128)(2,1)S(1)}, u32[]{:S(2)}, u32[]{:S(2)}) collective-permute-start(bf16[192,2048]{1,0:T(8,128)(2,1)S(1)} %get-tuple-element.153), channel_id=1, source_target_pairs={{0,8},{24,16},{1,9},{25,17},{2,10},{26,18},{3,11},{27,19},{4,12},{... | collective-permute-start | bytes 2359304 | tf_op jit(solution)/shard_map/ppermute | solution.py:231
  155.2 15.8 %collective-permute-start.32 = (bf16[384,512]{1,0:T(8,128)(2,1)S(1)}, bf16[384,512]{1,0:T(8,128)(2,1)S(1)}, u32[]{:S(2)}, u32[]{:S(2)}) collective-permute-start(bf16[384,512]{1,0:T(8,128)(2,1)S(1)} %encode.7.refs_2_), channel_id=1, source_target_pairs={{0,4},{4,0},{2,6},{6,2},{1,5},{5,1},{3,7},{7,3},{8,12},{12,8},{10,... | collective-permute-start | bytes 1179656 | tf_op jit(solution)/shard_map/ppermute | solution.py:222
  157.3 13.7 %collective-permute-start.33 = (bf16[384,512]{1,0:T(8,128)(2,1)S(1)}, bf16[384,512]{1,0:T(8,128)(2,1)S(1)}, u32[]{:S(2)}, u32[]{:S(2)}) collective-permute-start(bf16[384,512]{1,0:T(8,128)(2,1)S(1)} %encode.7.refs_2_), channel_id=1, source_target_pairs={{0,6},{6,0},{2,4},{4,2},{1,7},{7,1},{3,5},{5,3},{8,14},{14,8},{10,... | collective-permute-start | bytes 1179656 | tf_op jit(solution)/shard_map/ppermute | solution.py:222
  165.3 13.1 %collective-permute-start.29 = (bf16[192,2048]{1,0:T(8,128)(2,1)S(1)}, bf16[192,2048]{1,0:T(8,128)(2,1)S(1)}, u32[]{:S(2)}, u32[]{:S(2)}) collective-permute-start(bf16[192,2048]{1,0:T(8,128)(2,1)S(1)} %add_convert_fusion.6), channel_id=1, source_target_pairs={{8,16},{16,8},{9,17},{17,9},{10,18},{18,10},{11,19},{19,11},{12,20... | collective-permute-start | bytes 2359304 | tf_op jit(solution)/shard_map/ppermute | solution.py:236
  175.1 15.0 %collective-permute-start.36 = (bf16[192,2048]{1,0:T(8,128)(2,1)S(1)}, bf16[192,2048]{1,0:T(8,128)(2,1)S(1)}, u32[]{:S(2)}, u32[]{:S(2)}) collective-permute-start(bf16[192,2048]{1,0:T(8,128)(2,1)S(1)} %get-tuple-element.157), channel_id=1, source_target_pairs={{0,8},{24,16},{1,9},{25,17},{2,10},{26,18},{3,11},{27,19},{4,12},{... | collective-permute-start | bytes 2359304 | tf_op jit(solution)/shard_map/ppermute | solution.py:231
  177.1 18.4 %collective-permute-start.35 = (bf16[192,2048]{1,0:T(8,128)(2,1)S(1)}, bf16[192,2048]{1,0:T(8,128)(2,1)S(1)}, u32[]{:S(2)}, u32[]{:S(2)}) collective-permute-start(bf16[192,2048]{1,0:T(8,128)(2,1)S(1)} %add_convert_fusion.5), channel_id=1, source_target_pairs={{8,0},{16,24},{9,1},{17,25},{10,2},{18,26},{11,3},{19,27},{12,4},{... | collective-permute-start | bytes 2359304 | tf_op jit(solution)/shard_map/ppermute | solution.py:241
  190.1 16.4 %collective-permute-start.37 = (bf16[192,2048]{1,0:T(8,128)(2,1)S(1)}, bf16[192,2048]{1,0:T(8,128)(2,1)S(1)}, u32[]{:S(2)}, u32[]{:S(2)}) collective-permute-start(bf16[192,2048]{1,0:T(8,128)(2,1)S(1)} %get-tuple-element.162), channel_id=1, source_target_pairs={{0,8},{24,16},{1,9},{25,17},{2,10},{26,18},{3,11},{27,19},{4,12},{... | collective-permute-start | bytes 2359304 | tf_op jit(solution)/shard_map/ppermute | solution.py:231
  207.8 18.6 %collective-permute-start.40 = (bf16[192,2048]{1,0:T(8,128)(2,1)S(1)}, bf16[192,2048]{1,0:T(8,128)(2,1)S(1)}, u32[]{:S(2)}, u32[]{:S(2)}) collective-permute-start(bf16[192,2048]{1,0:T(8,128)(2,1)S(1)} %add_convert_fusion.1), channel_id=1, source_target_pairs={{8,0},{16,24},{9,1},{17,25},{10,2},{18,26},{11,3},{19,27},{12,4},{... | collective-permute-start | bytes 2359304 | tf_op jit(solution)/shard_map/ppermute | solution.py:241
  (20 other events, 173.5 us)

commit v2 on v1

--- a/solution.py
+++ b/solution.py
@@ -6,17 +6,20 @@
 from jax.sharding import PartitionSpec as P
 
 SIXTHS = (12, 12)
+DIRECT = ''
 ORDER = (
-    "named.0", "x.0", "all.0", "b1.0", "setup.0", "x.1", "wa1.0", "b2.0", "b1.1", "a1.1", "c2.0",
-    "ena.0", "c3.0", "c1.1", "b2.1", "wc2.0", "c2.1", "dea.0", "wc3.0", "s1.0", "enb.0", "wb2.1",
-    "wc1.1", "c3.1", "ena.1", "ws1.0", "wc2.1", "deb.0", "s3.0", "s2.0", "dea.1", "wc3.1", "s1.1",
-    "enb.1", "t2.0", "t1.0", "deb.1", "s3.1", "wt2.0", "ws1.1", "u1.0", "s2.1", "wt1.0", "t2.1",
-    "fin.0", "t1.1", "u1.1", "wt1.1", "fin.1",
+    "x.0", "all.0", "b1.0", "x.1", "named.0", "wa1.0", "wb1.0", "b2.0", "c2.0", "setup.0", "wset.0",
+    "a1.1", "b1.1", "ena.0", "c3.0", "wc2.0", "ma.0", "b2.1", "c1.1", "dea.0", "s1.0", "wc3.0",
+    "enb.0", "c2.1", "mb.0", "wc1.1", "ena.1", "ws1.0", "c3.1", "deb.0", "s3.0", "s2.0", "wc2.1",
+    "ma.1", "dea.1", "s1.1", "t2.0", "wc3.1", "enf.1", "t1.0", "u1.0", "mf.1", "wxf.1", "def.1",
+    "s3p.1", "s2p.1", "s3q.1", "s2q.1", "ws1.1", "fin.0", "t2p.1", "t1p.1", "u1p.1", "t2q.1",
+    "t1q.1", "u1q.1", "fin.1",
 )
 TO_MID = [(0, 1), (3, 2)]
 ACROSS = [(1, 2), (2, 1)]
 TO_END = [(1, 0), (2, 3)]
 SWAP = [(0, 1), (1, 0)]
+X_TP, Y_TP, FAR_TP = [(0, 1), (1, 0), (2, 3), (3, 2)], [(0, 2), (2, 0), (1, 3), (3, 1)], [(0, 3), (3, 0), (1, 2), (2, 1)]
 BF = jnp.bfloat16
 F32 = jnp.float32
 WSPEC = pl.BlockSpec(memory_space=pltpu.VMEM)
@@ -66,17 +69,18 @@
                 out[rs, k * bw:(k + 1) * bw] = a.astype(BF)
 
 
-def decode_kernel(slots, off, s_ref, pos, own, px, py, pd, bo, bp, wo, wp, *refs):
-    outs, codes = refs[:-1], refs[-1]
+def decode_kernel(slots, off, count, s_ref, pos, *refs):
+    parts, (bo, bp, wo, wp), outs, codes = refs[:count], refs[count:count + 4], refs[count + 4:-1], refs[-1]
+    own = parts[0]
     top = pos.shape[2]
     bw = own.shape[1] // top
-    r = outs[0].shape[0]
+    r = own.shape[0] // len(slots)
     h, width = wo.shape
     for i, slot in enumerate(slots):
         p = pos[s_ref[3 + slot], off:off + r, :]
         rs = slice(i * r, (i + 1) * r)
         wide = [jnp.broadcast_to(p[:, k:k + 1], (r, bw)) for k in range(top)]
-        tot = [own[rs, c].astype(F32) + px[rs, c].astype(F32) + (py[rs, c].astype(F32) + pd[rs, c].astype(F32))
+        tot = [sum(p_[rs, c].astype(F32) for p_ in parts)
                for c in (slice(k * bw, (k + 1) * bw) for k in range(top))]
         for bias, base, at in ((bo, s_ref[1], 0), (bp, s_ref[2], h)):
             for b in range(h // bw):
@@ -89,10 +93,19 @@
         c = slice(n * tile, (n + 1) * tile)
         y = jnp.dot(codes[:, :h], wo[:, c], preferred_element_type=F32) + jnp.dot(
             codes[:, h:], wp[:, c], preferred_element_type=F32)
-        for i, o in enumerate(outs):
-            o[:, c] = y[i * r:(i + 1) * r].astype(o.dtype)
-
-
+        row = 0
+        for o in outs:
+            o[:, c] = y[row:row + o.shape[0]].astype(o.dtype)
+            row += o.shape[0]
+
+
+GROUPS = {
+    "a": (("x", "c1"), ("x", "b1"), (0, 1), ("y0", "y1")),
+    "b": (("c2", "c3"), ("b2", "a1"), (2, 3), ("y2", "y3")),
+    "d": (("c2",), ("b2",), (2,), ("y2",)),
+    "f": (("c2", "c3"), ("b2", "a1"), (2, 3), ("y2p", "y2q", "y3p", "y3q")),
+    "e": (("c3",), ("a1",), (3,), ("y3p", "y3q")),
+}
 NEAR, FAR = pl.BlockSpec(memory_space=pltpu.VMEM), pl.BlockSpec(memory_space=pl.ANY)
 
 
@@ -113,15 +126,15 @@
     )(scal, pos, *at_end, *at_mid, wo, wp)
 
 
-def decode(scal, pos, off, slots, kinds, parts, bo, bp, wo, wp):
+def decode(scal, pos, off, slots, kinds, parts, bo, bp, wo, wp, cut=1):
     n = len(slots)
     r = parts[0].shape[0] // n
     half, width = wo.shape
     return pl.pallas_call(
-        lambda *refs: decode_kernel(slots, off, *refs),
-        out_shape=[jax.ShapeDtypeStruct((r, width), kind) for kind in kinds],
-        in_specs=[pl.BlockSpec(memory_space=pltpu.SMEM)] + [NEAR] * 7 + [WSPEC] * 2,
-        out_specs=[NEAR] * n,
+        lambda *refs: decode_kernel(slots, off, len(parts), *refs),
+        out_shape=[jax.ShapeDtypeStruct((r // cut, width), kind) for kind in kinds for _ in range(cut)],
+        in_specs=[pl.BlockSpec(memory_space=pltpu.SMEM)] + [NEAR] * (3 + len(parts)) + [WSPEC] * 2,
+        out_specs=[NEAR] * (len(kinds) * cut),
         scratch_shapes=[pltpu.VMEM((n * r, 2 * half), BF)],
         compiler_params=pltpu.CompilerParams(vmem_limit_bytes=VMEM),
         cost_estimate=pl.CostEstimate(flops=1, bytes_accessed=1, transcendentals=0),
@@ -160,6 +173,14 @@
         d.update(zip(names, vals))
         mark(*vals)
 
+    def part(d, n, q):
+        if f"y{n}{q}" in d:
+            return d[f"y{n}{q}"]
+        if not q:
+            return jnp.concatenate([d[f"y{n}p"], d[f"y{n}q"]])
+        half = d[f"y{n}"].shape[0] // 2
+        return d[f"y{n}"][:half] if q == "p" else d[f"y{n}"][half:]
+
     def named():
         ids = jnp.arange(nblocks, dtype=jnp.int32)
         pos = jnp.sum(jnp.where(active[:, :, None] == ids, placement_map, 0), axis=2)
@@ -189,6 +210,8 @@
             d["a1"] = d["c1"] = pp(after(d["x"])[0], "seq", TO_MID + TO_END)
         elif name == "setup":
             setup()
+        elif name == "wset":
+            wait(m, "ep", "dp", "bp")
         elif name == "named":
             named()
         elif name == "a1":
@@ -206,42 +229,52 @@
         elif name == "c3":
             wait(d, "b2")
             d["c3"] = pp(d["b2"], "seq", TO_END)
-        elif name in ("wxa", "wxb"):
-            wait(d, *["p" + name[2] + n for n in ("d", "x", "y")])
+        elif name[:2] == "wx":
+            wait(d, *["p" + name[2] + n for n in (("d", "x", "y") if name[2] in DIRECT else ("y",))])
         elif name[0] == "w":
             wait(d, name[1:])
-        elif name in ("ena", "enb"):
+        elif name[:2] == "en":
             h = name[2]
-            ends, mids, slots = (("x", "c1"), ("x", "b1"), (0, 1)) if h == "a" else (("c2", "c3"), ("b2", "a1"), (2, 3))
+            ends, mids, slots, _ = GROUPS[h]
             rows = after(*[d[n] for n in ends + mids])
-            pb = encode(m["scal"], m["pos"], offs[c], slots, rows[:2], rows[2:], enc_weight, m["ep"], bw)
+            pb = encode(m["scal"], m["pos"], offs[c], slots, rows[:len(ends)], rows[len(ends):], enc_weight, m["ep"], bw)
             mark(pb)
             d["p" + h] = pb
-            for n, p in (("d", [(0, 3), (3, 0), (1, 2), (2, 1)]), ("x", [(0, 1), (1, 0), (2, 3), (3, 2)]),
-                         ("y", [(0, 2), (2, 0), (1, 3), (3, 1)])):
-                d["p" + h + n] = pp(pb, "tp", p)
-        elif name in ("dea", "deb"):
+            if h in DIRECT:
+                for n, p in (("d", FAR_TP), ("x", X_TP), ("y", Y_TP)):
+                    d["p" + h + n] = pp(pb, "tp", p)
+            else:
+                d["p" + h + "x"] = pp(pb, "tp", X_TP)
+        elif name[0] == "m":
+            h = name[1]
+            wait(d, "p" + h + "x")
+            d["p" + h] = (f32(d["p" + h]) + f32(d["p" + h + "x"])).astype(BF)
+            mark(d["p" + h])
+            d["p" + h + "y"] = pp(d["p" + h], "tp", Y_TP)
+        elif name[:2] == "de":
             h = name[2]
-            parts = after(*[d["p" + h + n] for n in ("", "x", "y", "d")])
-            slots, kinds, ys = ((0, 1), (F32, BF), ("y0", "y1")) if h == "a" else ((2, 3), (BF, BF), ("y2", "y3"))
-            out = decode(m["scal"], m["pos"], offs[c], slots, kinds, parts, m["bo"], m["bp"], dec_weight, m["dp"])
+            parts = after(*[d["p" + h + n] for n in (("", "x", "y", "d") if h in DIRECT else ("", "y"))])
+            _, _, slots, ys = GROUPS[h]
+            kinds = [F32 if n == 0 else BF for n in slots]
+            out = decode(m["scal"], m["pos"], offs[c], slots, kinds, parts, m["bo"], m["bp"], dec_weight, m["dp"],
+                         len(ys) // len(slots))
             mark(*out)
             d.update(zip(ys, out))
-        elif name in ("s3", "s2", "s1"):
-            d[name] = pp(after(d["y" + name[1]])[0], "seq", TO_MID)
-        elif name in ("t2", "t1"):
-            wait(d, "s3" if name == "t2" else "s2")
-            z = (f32(d["y" + name[1]]) + f32(d["s3" if name == "t2" else "s2"])).astype(BF)
+        elif name[0] == "s":
+            d[name] = pp(after(part(d, name[1], name[2:]))[0], "seq", TO_MID)
+        elif name[0] in "tu":
+            n, q = name[1], name[2:]
+            src = ("s3" if n == "2" else "s2") if name[0] == "t" else "t2"
+            wait(d, src + q)
+            y = part(d, n if name[0] == "t" else "3", q)
+            z = (f32(y) + f32(d[src + q])).astype(BF)
             mark(z)
-            d[name] = pp(z, "seq", ACROSS)
-        elif name == "u1":
-            wait(d, "t2")
-            z = (f32(d["y3"]) + f32(d["t2"])).astype(BF)
-            mark(z)
-            d[name] = pp(z, "seq", TO_END)
+            d[name] = pp(z, "seq", ACROSS if name[0] == "t" else TO_END)
         elif name == "fin":
-            wait(d, "s1", "t1", "u1")
-            d["out"] = (d["y0"] + (f32(d["s1"]) + f32(d["t1"]) + f32(d["u1"])) + dec_bias[None, :]).astype(BF)
+            got = [[n] if n in d else [n + "p", n + "q"] for n in ("s1", "t1", "u1")]
+            wait(d, *sum(got, []))
+            s1, t1, u1 = [jnp.concatenate([f32(d[n]) for n in g]) for g in got]
+            d["out"] = (d["y0"] + (s1 + t1 + u1) + dec_bias[None, :]).astype(BF)
             mark(d["out"])
         else:
             raise ValueError(name)

time: 229 us -> 210 us (0.917)
  waiting for transfers between devices: 112 us -> 91.5 us
  local copies, waits for them, and re-layouts: 7.68 us -> 1.46 us
  Pallas kernels: 30.7 us -> 35.9 us
    ppermute x24 -> x25, waiting for transfers between devices: 79.1 us -> 55.7 us  [the longest x8 31.7 us: step(): d[name] = pp(after(part(d, name[1], name[2:]))[0], 'seq', TO_MID)]
    ppermute x1, waiting for transfers between devices: 16.9 us -> 0.01 us  [step(): d['a1'] = d['c1'] = pp(after(d['x'])[0], 'seq', TO_MID + TO_END)]
    ppermute x3, waiting for transfers between devices: 0.57 us -> 13.5 us  [named(): m[f'n{k}'] = pp(pos, 'seq', [(i, (i + k) % nseq) for i in range(nseq)])]
    ppermute x2, waiting for transfers between devices: 12.4 us -> 4.85 us  [step(): d['c2'] = pp(d['b1'], 'seq', TO_END)]
    ppermute x1, waiting for transfers between devices: 1.15 us -> 7.66 us  [step(): d['a1'] = pp(after(d['x'])[0], 'seq', TO_MID)]
    ppermute x1, waiting for transfers between devices: 0.32 us -> 4.87 us  [step(): d['c1'] = pp(after(d['x'])[0], 'seq', TO_END)]
    unnamed x22 -> x16, local copies, waits for them, and re-layouts: 5.7 us -> 1.17 us
    ppermute x1, starting transfers between devices: 5.69 us -> 2.62 us  [step(): d['a1'] = pp(after(d['x'])[0], 'seq', TO_MID)]
  transfers between devices with their start and end apart: 41 -> 42, of which waited for: 19 -> 22; matrix products, arithmetic and copies ran while one was open for 3% -> 2% of each run, Pallas kernels for 13% -> 17%
where the time goes in v2:
time: 210 us; the launch traced here: 209 us
  waiting for transfers between devices  91.5 us (44%)
  starting transfers between devices  71.9 us (34%)
  Pallas kernels  35.9 us (17%)
  other arithmetic  7.26 us (3%)
    ppermute x8, waiting for transfers between devices, step(): d[name] = pp(after(part(d, name[1], name[2:]))[0], 'seq', TO_MID)  31.7 us
    ppermute x8, starting transfers between devices, step(): d[name] = pp(after(part(d, name[1], name[2:]))[0], 'seq', TO_MID)  28.2 us
    pallas_call x4, Pallas kernels, decode(): pl.pallas_call(lambda *refs: decode_kernel(slots, off, len(parts), *refs)...  18.6 us
    pallas_call x4, Pallas kernels, encode(): pl.pallas_call(lambda *refs: encode_kernel(slots, off, *refs), out_shape=...  17.3 us
    ppermute x9, waiting for transfers between devices, step(): d[name] = pp(z, 'seq', ACROSS if name[0] == 't' else TO_END)  15 us
    ppermute x3, waiting for transfers between devices, named(): m[f'n{k}'] = pp(pos, 'seq', [(i, (i + k) % nseq) for i in range(nseq)])  13.5 us
    ppermute x9, starting transfers between devices, step(): d[name] = pp(z, 'seq', ACROSS if name[0] == 't' else TO_END)  8.04 us
    ppermute x1, waiting for transfers between devices, step(): d['a1'] = pp(after(d['x'])[0], 'seq', TO_MID)  7.66 us
  transfers between devices with their start and end apart: 42, of which 22 were waited for; matrix products, arithmetic and copies ran while one was open for 2% of the time, Pallas kernels for 17%

profile of v2, /device:TPU:0, one launch (start us, length us, event | category | flops | bytes accessed | tf_op | source)
XLA Modules:
  0.0 208.6 jit_solution(14885761259097455150)
XLA Ops:
  1.4 3.1 %collective-permute-start.3 = (bf16[192,2048]{1,0:T(8,128)(2,1)S(1)}, bf16[192,2048]{1,0:T(8,128)(2,1)}, u32[]{:S(2)}, u32[]{:S(2)}) collective-permute-start(bf16[192,2048]{1,0:T(8,128)(2,1)S(1)} %subtract_convert_fusion.1.refs_2_.refs_4_), channel_id=1, source_target_pairs={{0,8},{24,16},{8,0},{16,24},{1,9},{25,17},{9,1},{17,25},{2,10},{26... | collective-permute-start | bytes 2359304 | tf_op jit(solution)/shard_map/ppermute | solution.py:210
  6.2 3.6 %collective-permute-start = (s32[384,4]{0,1:T(4,128)S(1)}, s32[384,4]{0,1:T(4,128)S(1)}, u32[]{:S(2)}, u32[]{:S(2)}) collective-permute-start(s32[384,4]{0,1:T(4,128)S(1)} %select_reduce_fusion), channel_id=1, source_target_pairs={{0,8},{8,16},{16,24},{24,0},{1,9},{9,17},{17,25},{25,1},{2,10},{10... | collective-permute-start | bytes 18440 | tf_op jit(solution)/shard_map/ppermute | solution.py:189
  9.8 2.4 %collective-permute-start.2 = (s32[384,4]{0,1:T(4,128)S(1)}, s32[384,4]{0,1:T(4,128)S(1)}, u32[]{:S(2)}, u32[]{:S(2)}) collective-permute-start(s32[384,4]{0,1:T(4,128)S(1)} %select_reduce_fusion), channel_id=1, source_target_pairs={{0,24},{8,0},{16,8},{24,16},{1,25},{9,1},{17,9},{25,17},{2,26},{10... | collective-permute-start | bytes 18440 | tf_op jit(solution)/shard_map/ppermute | solution.py:189
  13.2 11.3 %collective-permute-done = s32[384,4]{0,1:T(4,128)S(1)} collective-permute-done((s32[384,4]{0,1:T(4,128)S(1)}, s32[384,4]{0,1:T(4,128)S(1)}, u32[]{:S(2)}, u32[]{:S(2)}) %collective-permute-start) | collective-permute-done | bytes 6176 | tf_op jit(solution)/shard_map/ppermute | solution.py:189
  24.6 2.1 %collective-permute-done.1 = s32[384,4]{0,1:T(4,128)S(1)} collective-permute-done((s32[384,4]{0,1:T(4,128)S(1)}, s32[384,4]{0,1:T(4,128)S(1)}, u32[]{:S(2)}, u32[]{:S(2)}) %collective-permute-start.1) | collective-permute-done | bytes 6176 | tf_op jit(solution)/shard_map/ppermute | solution.py:189
  27.3 1.6 collective-permute-start.10
  31.4 2.1 %collective-permute-done.7.refs_5_ = f32[1,512]{1,0:T(1,128)S(1)} collective-permute-done((f32[1,512]{1,0:T(1,128)S(1)}, f32[1,512]{1,0:T(1,128)S(1)}, u32[]{:S(2)}, u32[]{:S(2)}) %collective-permute-start.7) | collective-permute-done | bytes 2080 | tf_op jit(solution)/shard_map/ppermute | solution.py:198
  35.4 4.9 %encode.4 = bf16[384,512]{1,0:T(8,128)(2,1)S(1)} custom-call(s32[7]{0:T(128)S(1)} %pad_add_fusion.1.refs_0_, s32[4,384,4]{2,1,0:T(8,128)S(1)} %copy.20.refs_1_, bf16[192,2048]{1,0:T(8,128)(2,1)S(1)} %copy-done.3, bf16[192,2048]{1,0:T(8,128)(2,1)} %collective-permute-done.3.refs_3_.refs_5_, bf16[192,2048]{1,0:T(8,128)(2,1)S(1)} %copy-done.3, ...), custom_call_target="tpu_custom_call" | custom-call | flops 1 | bytes 1 | tf_op jit(solution)/shard_map/encode/pallas_call | solution.py:117
  41.9 2.6 %collective-permute-start.12 = (bf16[192,2048]{1,0:T(8,128)(2,1)S(1)}, bf16[192,2048]{1,0:T(8,128)(2,1)S(1)}, u32[]{:S(2)}, u32[]{:S(2)}) collective-permute-start(bf16[192,2048]{1,0:T(8,128)(2,1)S(1)} %copy-done.1), channel_id=1, source_target_pairs={{0,8},{24,16},{1,9},{25,17},{2,10},{26,18},{3,11},{27,19},{4,12},{... | collective-permute-start | bytes 2359304 | tf_op jit(solution)/shard_map/ppermute | solution.py:218
  45.8 4.8 %collective-permute-done.9.refs_2_ = bf16[192,2048]{1,0:T(8,128)(2,1)} collective-permute-done((bf16[192,2048]{1,0:T(8,128)(2,1)}, bf16[192,2048]{1,0:T(8,128)(2,1)}, u32[]{:S(2)}, u32[]{:S(2)}) %collective-permute-start.9) | collective-permute-done | bytes 786464 | tf_op jit(solution)/shard_map/ppermute | solution.py:228
  53.9 7.7 %collective-permute-done.12.refs_5_ = bf16[192,2048]{1,0:T(8,128)(2,1)S(1)} collective-permute-done((bf16[192,2048]{1,0:T(8,128)(2,1)S(1)}, bf16[192,2048]{1,0:T(8,128)(2,1)S(1)}, u32[]{:S(2)}, u32[]{:S(2)}) %collective-permute-start.12) | collective-permute-done | bytes 786464 | tf_op jit(solution)/shard_map/ppermute | solution.py:218
  62.0 4.7 %decode.4 = (f32[192,2048]{1,0:T(8,128)S(1)}, bf16[192,2048]{1,0:T(8,128)(2,1)S(1)}) custom-call(s32[7]{0:T(128)S(1)} %pad_add_fusion.1.refs_0_, s32[4,384,4]{2,1,0:T(8,128)S(1)} %copy.20.refs_1_, bf16[384,512]{1,0:T(8,128)(2,1)S(1)} %add_convert_fusion.14.refs_2_, bf16[384,512]{1,0:T(8,128)(2,1)S(1)} %collective-permute-done.11.refs_3_, ...), custom_call_target="tpu_custom_call" | custom-call | flops 1 | bytes 1 | tf_op jit(solution)/shard_map/decode/pallas_call | solution.py:133
  69.3 4.8 %encode.5 = bf16[384,512]{1,0:T(8,128)(2,1)S(1)} custom-call(s32[7]{0:T(128)S(1)} %pad_add_fusion.1.refs_0_, s32[4,384,4]{2,1,0:T(8,128)S(1)} %copy.20.refs_1_, bf16[192,2048]{1,0:T(8,128)(2,1)} %collective-permute-done.9.refs_2_, bf16[192,2048]{1,0:T(8,128)(2,1)S(1)} %collective-permute-done.15.refs_3_, bf16[192,2048]{1,0:T(8,128)(2,1)} %collective-permute-done.10.refs_4_, ...), custom_call_target="tpu_custom_call" | custom-call | flops 1 | bytes 1 | tf_op jit(solution)/shard_map/encode/pallas_call | solution.py:117
  75.7 4.9 %collective-permute-start.13 = (bf16[192,2048]{1,0:T(8,128)(2,1)S(1)}, bf16[192,2048]{1,0:T(8,128)(2,1)S(1)}, u32[]{:S(2)}, u32[]{:S(2)}) collective-permute-start(bf16[192,2048]{1,0:T(8,128)(2,1)S(1)} %get-tuple-element.123), channel_id=1, source_target_pairs={{0,8},{24,16},{1,9},{25,17},{2,10},{26,18},{3,11},{27,19},{4,12},{... | collective-permute-start | bytes 2359304 | tf_op jit(solution)/shard_map/ppermute | solution.py:264
  85.5 4.9 %collective-permute-done.14.refs_3_ = bf16[192,2048]{1,0:T(8,128)(2,1)S(1)} collective-permute-done((bf16[192,2048]{1,0:T(8,128)(2,1)S(1)}, bf16[192,2048]{1,0:T(8,128)(2,1)S(1)}, u32[]{:S(2)}, u32[]{:S(2)}) %collective-permute-start.14) | collective-permute-done | bytes 786464 | tf_op jit(solution)/shard_map/ppermute | solution.py:222
  90.4 3.8 %encode.6 = bf16[384,512]{1,0:T(8,128)(2,1)S(1)} custom-call(s32[7]{0:T(128)S(1)} %pad_add_fusion.1.refs_0_, s32[4,384,4]{2,1,0:T(8,128)S(1)} %copy.20.refs_1_, bf16[192,2048]{1,0:T(8,128)(2,1)S(1)} %copy-done.1, bf16[192,2048]{1,0:T(8,128)(2,1)S(1)} %collective-permute-done.14.refs_3_, bf16[192,2048]{1,0:T(8,128)(2,1)S(1)} %copy-done.1, ...), custom_call_target="tpu_custom_call" | custom-call | flops 1 | bytes 1 | tf_op jit(solution)/shard_map/encode/pallas_call | solution.py:117
  95.8 4.7 %decode.5 = (bf16[192,2048]{1,0:T(8,128)(2,1)S(1)}, bf16[192,2048]{1,0:T(8,128)(2,1)S(1)}) custom-call(s32[7]{0:T(128)S(1)} %pad_add_fusion.1.refs_0_, s32[4,384,4]{2,1,0:T(8,128)S(1)} %copy.20.refs_1_, bf16[384,512]{1,0:T(8,128)(2,1)S(1)} %add_convert_fusion.13.refs_2_, bf16[384,512]{1,0:T(8,128)(2,1)S(1)} %collective-permute-done.18.refs_3_, ...), custom_call_target="tpu_custom_call" | custom-call | flops 1 | bytes 1 | tf_op jit(solution)/shard_map/decode/pallas_call | solution.py:133
  100.5 5.5 %collective-permute-start.23 = (bf16[192,2048]{1,0:T(8,128)(2,1)S(1)}, bf16[192,2048]{1,0:T(8,128)(2,1)S(1)}, u32[]{:S(2)}, u32[]{:S(2)}) collective-permute-start(bf16[192,2048]{1,0:T(8,128)(2,1)S(1)} %get-tuple-element.145), channel_id=1, source_target_pairs={{0,8},{24,16},{1,9},{25,17},{2,10},{26,18},{3,11},{27,19},{4,12},{... | collective-permute-start | bytes 2359304 | tf_op jit(solution)/shard_map/ppermute | solution.py:264
  109.0 4.8 %collective-permute-start.20 = (bf16[192,2048]{1,0:T(8,128)(2,1)S(1)}, bf16[192,2048]{1,0:T(8,128)(2,1)S(1)}, u32[]{:S(2)}, u32[]{:S(2)}) collective-permute-start(bf16[192,2048]{1,0:T(8,128)(2,1)S(1)} %get-tuple-element.143), channel_id=1, source_target_pairs={{0,8},{24,16},{1,9},{25,17},{2,10},{26,18},{3,11},{27,19},{4,12},{... | collective-permute-start | bytes 2359304 | tf_op jit(solution)/shard_map/ppermute | solution.py:264
  114.0 4.7 %decode.6 = (f32[192,2048]{1,0:T(8,128)S(1)}, bf16[192,2048]{1,0:T(8,128)(2,1)S(1)}) custom-call(s32[7]{0:T(128)S(1)} %pad_add_fusion.1.refs_0_, s32[4,384,4]{2,1,0:T(8,128)S(1)} %copy.20.refs_1_, bf16[384,512]{1,0:T(8,128)(2,1)S(1)} %add_convert_fusion.12.refs_2_, bf16[384,512]{1,0:T(8,128)(2,1)S(1)} %collective-permute-done.25.refs_3_, ...), custom_call_target="tpu_custom_call" | custom-call | flops 1 | bytes 1 | tf_op jit(solution)/shard_map/decode/pallas_call | solution.py:133
  118.7 5.2 %collective-permute-done.23 = bf16[192,2048]{1,0:T(8,128)(2,1)S(1)} collective-permute-done((bf16[192,2048]{1,0:T(8,128)(2,1)S(1)}, bf16[192,2048]{1,0:T(8,128)(2,1)S(1)}, u32[]{:S(2)}, u32[]{:S(2)}) %collective-permute-start.23) | collective-permute-done | bytes 786464 | tf_op jit(solution)/shard_map/ppermute | solution.py:264
  125.6 3.8 %encode.7 = bf16[384,512]{1,0:T(8,128)(2,1)S(1)} custom-call(s32[7]{0:T(128)S(1)} %pad_add_fusion.1.refs_0_, s32[4,384,4]{2,1,0:T(8,128)S(1)} %copy.20.refs_1_, bf16[192,2048]{1,0:T(8,128)(2,1)S(1)} %collective-permute-done.21.refs_2_, bf16[192,2048]{1,0:T(8,128)(2,1)S(1)} %collective-permute-done.22.refs_3_, ...), custom_call_target="tpu_custom_call" | custom-call | flops 1 | bytes 1 | tf_op jit(solution)/shard_map/encode/pallas_call | solution.py:117
  130.6 6.2 %collective-permute-done.20 = bf16[192,2048]{1,0:T(8,128)(2,1)S(1)} collective-permute-done((bf16[192,2048]{1,0:T(8,128)(2,1)S(1)}, bf16[192,2048]{1,0:T(8,128)(2,1)S(1)}, u32[]{:S(2)}, u32[]{:S(2)}) %collective-permute-start.20) | collective-permute-done | bytes 786464 | tf_op jit(solution)/shard_map/ppermute | solution.py:264
  136.8 4.4 %collective-permute-start.29 = (bf16[192,2048]{1,0:T(8,128)(2,1)S(1)}, bf16[192,2048]{1,0:T(8,128)(2,1)S(1)}, u32[]{:S(2)}, u32[]{:S(2)}) collective-permute-start(bf16[192,2048]{1,0:T(8,128)(2,1)S(1)} %get-tuple-element.159), channel_id=1, source_target_pairs={{0,8},{24,16},{1,9},{25,17},{2,10},{26,18},{3,11},{27,19},{4,12},{... | collective-permute-start | bytes 2359304 | tf_op jit(solution)/shard_map/ppermute | solution.py:264
  145.5 6.3 %collective-permute-done.31.refs_3_ = bf16[384,512]{1,0:T(8,128)(2,1)S(1)} collective-permute-done((bf16[384,512]{1,0:T(8,128)(2,1)S(1)}, bf16[384,512]{1,0:T(8,128)(2,1)S(1)}, u32[]{:S(2)}, u32[]{:S(2)}) %collective-permute-start.31) | collective-permute-done | bytes 393248 | tf_op jit(solution)/shard_map/ppermute | solution.py:253
  151.8 4.7 %decode.7 = (bf16[96,2048]{1,0:T(8,128)(2,1)S(1)}, bf16[96,2048]{1,0:T(8,128)(2,1)S(1)}, bf16[96,2048]{1,0:T(8,128)(2,1)S(1)}, bf16[96,2048]{1,0:T(8,128)(2,1)S(1)}) custom-call(s32[7]{0:T(128)S(1)} %pad_add_fusion.1.refs_0_, s32[4,384,4]{2,1,0:T(8,128)S(1)} %copy.20.refs_1_, bf16[384,512]{1,0:T(8,128)(2,1)S(1)} %add_convert_fusion.11.refs_2_, ...), custom_call_target="tpu_custom_call" | custom-call | flops 1 | bytes 1 | tf_op jit(solution)/shard_map/decode/pallas_call | solution.py:133
  156.5 4.6 %collective-permute-start.33 = (bf16[96,2048]{1,0:T(8,128)(2,1)S(1)}, bf16[96,2048]{1,0:T(8,128)(2,1)S(1)}, u32[]{:S(2)}, u32[]{:S(2)}) collective-permute-start(bf16[96,2048]{1,0:T(8,128)(2,1)S(1)} %get-tuple-element.173), channel_id=1, source_target_pairs={{0,8},{24,16},{1,9},{25,17},{2,10},{26,18},{3,11},{27,19},{4,12},{... | collective-permute-start | bytes 1179656 | tf_op jit(solution)/shard_map/ppermute | solution.py:264
  165.6 5.1 %collective-permute-done.33 = bf16[96,2048]{1,0:T(8,128)(2,1)S(1)} collective-permute-done((bf16[96,2048]{1,0:T(8,128)(2,1)S(1)}, bf16[96,2048]{1,0:T(8,128)(2,1)S(1)}, u32[]{:S(2)}, u32[]{:S(2)}) %collective-permute-start.33) | collective-permute-done | bytes 393248 | tf_op jit(solution)/shard_map/ppermute | solution.py:264
  171.4 7.6 %collective-permute-done.32 = bf16[96,2048]{1,0:T(8,128)(2,1)S(1)} collective-permute-done((bf16[96,2048]{1,0:T(8,128)(2,1)S(1)}, bf16[96,2048]{1,0:T(8,128)(2,1)S(1)}, u32[]{:S(2)}, u32[]{:S(2)}) %collective-permute-start.32) | collective-permute-done | bytes 393248 | tf_op jit(solution)/shard_map/ppermute | solution.py:264
  181.3 4.2 %collective-permute-done.36 = bf16[96,2048]{1,0:T(8,128)(2,1)S(1)} collective-permute-done((bf16[96,2048]{1,0:T(8,128)(2,1)S(1)}, bf16[96,2048]{1,0:T(8,128)(2,1)S(1)}, u32[]{:S(2)}, u32[]{:S(2)}) %collective-permute-start.36) | collective-permute-done | bytes 393248 | tf_op jit(solution)/shard_map/ppermute | solution.py:264
  186.2 3.4 %collective-permute-done.35 = bf16[96,2048]{1,0:T(8,128)(2,1)S(1)} collective-permute-done((bf16[96,2048]{1,0:T(8,128)(2,1)S(1)}, bf16[96,2048]{1,0:T(8,128)(2,1)S(1)}, u32[]{:S(2)}, u32[]{:S(2)}) %collective-permute-start.35) | collective-permute-done | bytes 393248 | tf_op jit(solution)/shard_map/ppermute | solution.py:264
  193.1 13.8 %collective-permute-done.41 = bf16[96,2048]{1,0:T(8,128)(2,1)S(1)} collective-permute-done((bf16[96,2048]{1,0:T(8,128)(2,1)S(1)}, bf16[96,2048]{1,0:T(8,128)(2,1)S(1)}, u32[]{:S(2)}, u32[]{:S(2)}) %collective-permute-start.41) | collective-permute-done | bytes 393248 | tf_op jit(solution)/shard_map/ppermute | solution.py:272
  (101 shorter events, 49.9 us)
Async XLA Ops:
  1.4 25.3 %collective-permute-start.3 = (bf16[192,2048]{1,0:T(8,128)(2,1)S(1)}, bf16[192,2048]{1,0:T(8,128)(2,1)}, u32[]{:S(2)}, u32[]{:S(2)}) collective-permute-start(bf16[192,2048]{1,0:T(8,128)(2,1)S(1)} %subtract_convert_fusion.1.refs_2_.refs_4_), channel_id=1, source_target_pairs={{0,8},{24,16},{8,0},{16,24},{1,9},{25,17},{9,1},{17,25},{2,10},{26... | collective-permute-start | bytes 2359304 | tf_op jit(solution)/shard_map/ppermute | solution.py:210
  4.5 22.2 %collective-permute-start.4 = (bf16[192,2048]{1,0:T(8,128)(2,1)S(1)}, bf16[192,2048]{1,0:T(8,128)(2,1)}, u32[]{:S(2)}, u32[]{:S(2)}) collective-permute-start(bf16[192,2048]{1,0:T(8,128)(2,1)S(1)} %subtract_convert_fusion.1.refs_2_.refs_4_), channel_id=1, source_target_pairs={{8,16},{16,8},{9,17},{17,9},{10,18},{18,10},{11,19},{19,11},{12,20... | collective-permute-start | bytes 2359304 | tf_op jit(solution)/shard_map/ppermute | solution.py:220
  6.2 18.4 %collective-permute-start = (s32[384,4]{0,1:T(4,128)S(1)}, s32[384,4]{0,1:T(4,128)S(1)}, u32[]{:S(2)}, u32[]{:S(2)}) collective-permute-start(s32[384,4]{0,1:T(4,128)S(1)} %select_reduce_fusion), channel_id=1, source_target_pairs={{0,8},{8,16},{16,24},{24,0},{1,9},{9,17},{17,25},{25,1},{2,10},{10... | collective-permute-start | bytes 18440 | tf_op jit(solution)/shard_map/ppermute | solution.py:189
  9.8 16.9 %collective-permute-start.1 = (s32[384,4]{0,1:T(4,128)S(1)}, s32[384,4]{0,1:T(4,128)S(1)}, u32[]{:S(2)}, u32[]{:S(2)}) collective-permute-start(s32[384,4]{0,1:T(4,128)S(1)} %select_reduce_fusion), channel_id=1, source_target_pairs={{0,16},{8,24},{16,0},{24,8},{1,17},{9,25},{17,1},{25,9},{2,18},{10... | collective-permute-start | bytes 18440 | tf_op jit(solution)/shard_map/ppermute | solution.py:189
  9.8 16.9 %collective-permute-start.2 = (s32[384,4]{0,1:T(4,128)S(1)}, s32[384,4]{0,1:T(4,128)S(1)}, u32[]{:S(2)}, u32[]{:S(2)}) collective-permute-start(s32[384,4]{0,1:T(4,128)S(1)} %select_reduce_fusion), channel_id=1, source_target_pairs={{0,24},{8,0},{16,8},{24,16},{1,25},{9,1},{17,9},{25,17},{2,26},{10... | collective-permute-start | bytes 18440 | tf_op jit(solution)/shard_map/ppermute | solution.py:189
  27.3 17.2 %collective-permute-start.10 = (bf16[192,2048]{1,0:T(8,128)(2,1)}, bf16[192,2048]{1,0:T(8,128)(2,1)}, u32[]{:S(2)}, u32[]{:S(2)}) collective-permute-start(bf16[192,2048]{1,0:T(8,128)(2,1)} %collective-permute-done.3.refs_3_.refs_5_), channel_id=1, source_target_pairs={{8,16},{16,8},{9,17},{17,9},{10,18},{18,10},{11,19},{19,11},{12,20... | collective-permute-start | bytes 2359304 | tf_op jit(solution)/shard_map/ppermute | solution.py:225
  28.9 21.7 %collective-permute-start.9 = (bf16[192,2048]{1,0:T(8,128)(2,1)}, bf16[192,2048]{1,0:T(8,128)(2,1)}, u32[]{:S(2)}, u32[]{:S(2)}) collective-permute-start(bf16[192,2048]{1,0:T(8,128)(2,1)} %collective-permute-done.4.refs_5_), channel_id=1, source_target_pairs={{8,0},{16,24},{9,1},{17,25},{10,2},{18,26},{11,3},{19,27},{12,4},{... | collective-permute-start | bytes 2359304 | tf_op jit(solution)/shard_map/ppermute | solution.py:228
  40.3 11.2 %collective-permute-start.8 = (bf16[384,512]{1,0:T(8,128)(2,1)S(1)}, bf16[384,512]{1,0:T(8,128)(2,1)S(1)}, u32[]{:S(2)}, u32[]{:S(2)}) collective-permute-start(bf16[384,512]{1,0:T(8,128)(2,1)S(1)} %encode.4), channel_id=1, source_target_pairs={{0,2},{2,0},{4,6},{6,4},{1,3},{3,1},{5,7},{7,5},{8,10},{10,8},{12,... | collective-permute-start | bytes 1179656 | tf_op jit(solution)/shard_map/ppermute | solution.py:247
  41.9 19.7 %collective-permute-start.12 = (bf16[192,2048]{1,0:T(8,128)(2,1)S(1)}, bf16[192,2048]{1,0:T(8,128)(2,1)S(1)}, u32[]{:S(2)}, u32[]{:S(2)}) collective-permute-start(bf16[192,2048]{1,0:T(8,128)(2,1)S(1)} %copy-done.1), channel_id=1, source_target_pairs={{0,8},{24,16},{1,9},{25,17},{2,10},{26,18},{3,11},{27,19},{4,12},{... | collective-permute-start | bytes 2359304 | tf_op jit(solution)/shard_map/ppermute | solution.py:218
  44.5 23.6 %collective-permute-start.15 = (bf16[192,2048]{1,0:T(8,128)(2,1)}, bf16[192,2048]{1,0:T(8,128)(2,1)S(1)}, u32[]{:S(2)}, u32[]{:S(2)}) collective-permute-start(bf16[192,2048]{1,0:T(8,128)(2,1)} %collective-permute-done.10.refs_4_), channel_id=1, source_target_pairs={{8,0},{16,24},{9,1},{17,25},{10,2},{18,26},{11,3},{19,27},{12,4},{... | collective-permute-start | bytes 2359304 | tf_op jit(solution)/shard_map/ppermute | solution.py:231
  53.2 28.1 %collective-permute-start.17 = (bf16[192,2048]{1,0:T(8,128)(2,1)S(1)}, bf16[192,2048]{1,0:T(8,128)(2,1)S(1)}, u32[]{:S(2)}, u32[]{:S(2)}) collective-permute-start(bf16[192,2048]{1,0:T(8,128)(2,1)S(1)} %copy-done.1), channel_id=1, source_target_pairs={{8,16},{16,8},{9,17},{17,9},{10,18},{18,10},{11,19},{19,11},{12,20... | collective-permute-start | bytes 2359304 | tf_op jit(solution)/shard_map/ppermute | solution.py:220
  68.1 22.4 %collective-permute-start.14 = (bf16[192,2048]{1,0:T(8,128)(2,1)S(1)}, bf16[192,2048]{1,0:T(8,128)(2,1)S(1)}, u32[]{:S(2)}, u32[]{:S(2)}) collective-permute-start(bf16[192,2048]{1,0:T(8,128)(2,1)S(1)} %copy-done.1), channel_id=1, source_target_pairs={{8,0},{16,24},{9,1},{17,25},{10,2},{18,26},{11,3},{19,27},{12,4},{... | collective-permute-start | bytes 2359304 | tf_op jit(solution)/shard_map/ppermute | solution.py:222
  75.7 20.1 %collective-permute-start.13 = (bf16[192,2048]{1,0:T(8,128)(2,1)S(1)}, bf16[192,2048]{1,0:T(8,128)(2,1)S(1)}, u32[]{:S(2)}, u32[]{:S(2)}) collective-permute-start(bf16[192,2048]{1,0:T(8,128)(2,1)S(1)} %get-tuple-element.123), channel_id=1, source_target_pairs={{0,8},{24,16},{1,9},{25,17},{2,10},{26,18},{3,11},{27,19},{4,12},{... | collective-permute-start | bytes 2359304 | tf_op jit(solution)/shard_map/ppermute | solution.py:264
  80.6 15.2 %collective-permute-start.19 = (bf16[192,2048]{1,0:T(8,128)(2,1)S(1)}, bf16[192,2048]{1,0:T(8,128)(2,1)S(1)}, u32[]{:S(2)}, u32[]{:S(2)}) collective-permute-start(bf16[192,2048]{1,0:T(8,128)(2,1)S(1)} %collective-permute-done.12.refs_5_), channel_id=1, source_target_pairs={{8,16},{16,8},{9,17},{17,9},{10,18},{18,10},{11,19},{19,11},{12,20... | collective-permute-start | bytes 2359304 | tf_op jit(solution)/shard_map/ppermute | solution.py:225
  81.3 24.6 %collective-permute-start.21 = (bf16[192,2048]{1,0:T(8,128)(2,1)S(1)}, bf16[192,2048]{1,0:T(8,128)(2,1)S(1)}, u32[]{:S(2)}, u32[]{:S(2)}) collective-permute-start(bf16[192,2048]{1,0:T(8,128)(2,1)S(1)} %collective-permute-done.17.refs_5_), channel_id=1, source_target_pairs={{8,0},{16,24},{9,1},{17,25},{10,2},{18,26},{11,3},{19,27},{12,4},{... | collective-permute-start | bytes 2359304 | tf_op jit(solution)/shard_map/ppermute | solution.py:228
  84.0 11.8 %collective-permute-start.18 = (bf16[384,512]{1,0:T(8,128)(2,1)S(1)}, bf16[384,512]{1,0:T(8,128)(2,1)S(1)}, u32[]{:S(2)}, u32[]{:S(2)}) collective-permute-start(bf16[384,512]{1,0:T(8,128)(2,1)S(1)} %add_convert_fusion.13.refs_2_), channel_id=1, source_target_pairs={{0,4},{4,0},{2,6},{6,2},{1,5},{5,1},{3,7},{7,3},{8,12},{12,8},{10,... | collective-permute-start | bytes 1179656 | tf_op jit(solution)/shard_map/ppermute | solution.py:253
  94.2 11.7 %collective-permute-start.24 = (bf16[384,512]{1,0:T(8,128)(2,1)S(1)}, bf16[384,512]{1,0:T(8,128)(2,1)S(1)}, u32[]{:S(2)}, u32[]{:S(2)}) collective-permute-start(bf16[384,512]{1,0:T(8,128)(2,1)S(1)} %encode.6), channel_id=1, source_target_pairs={{0,2},{2,0},{4,6},{6,4},{1,3},{3,1},{5,7},{7,5},{8,10},{10,8},{12,... | collective-permute-start | bytes 1179656 | tf_op jit(solution)/shard_map/ppermute | solution.py:247
  100.5 23.4 %collective-permute-start.23 = (bf16[192,2048]{1,0:T(8,128)(2,1)S(1)}, bf16[192,2048]{1,0:T(8,128)(2,1)S(1)}, u32[]{:S(2)}, u32[]{:S(2)}) collective-permute-start(bf16[192,2048]{1,0:T(8,128)(2,1)S(1)} %get-tuple-element.145), channel_id=1, source_target_pairs={{0,8},{24,16},{1,9},{25,17},{2,10},{26,18},{3,11},{27,19},{4,12},{... | collective-permute-start | bytes 2359304 | tf_op jit(solution)/shard_map/ppermute | solution.py:264
  107.7 17.9 %collective-permute-start.22 = (bf16[192,2048]{1,0:T(8,128)(2,1)S(1)}, bf16[192,2048]{1,0:T(8,128)(2,1)S(1)}, u32[]{:S(2)}, u32[]{:S(2)}) collective-permute-start(bf16[192,2048]{1,0:T(8,128)(2,1)S(1)} %collective-permute-done.19.refs_4_), channel_id=1, source_target_pairs={{8,0},{16,24},{9,1},{17,25},{10,2},{18,26},{11,3},{19,27},{12,4},{... | collective-permute-start | bytes 2359304 | tf_op jit(solution)/shard_map/ppermute | solution.py:231
  109.0 27.9 %collective-permute-start.20 = (bf16[192,2048]{1,0:T(8,128)(2,1)S(1)}, bf16[192,2048]{1,0:T(8,128)(2,1)S(1)}, u32[]{:S(2)}, u32[]{:S(2)}) collective-permute-start(bf16[192,2048]{1,0:T(8,128)(2,1)S(1)} %get-tuple-element.143), channel_id=1, source_target_pairs={{0,8},{24,16},{1,9},{25,17},{2,10},{26,18},{3,11},{27,19},{4,12},{... | collective-permute-start | bytes 2359304 | tf_op jit(solution)/shard_map/ppermute | solution.py:264
  124.2 18.1 %collective-permute-start.27 = (bf16[192,2048]{1,0:T(8,128)(2,1)S(1)}, bf16[192,2048]{1,0:T(8,128)(2,1)S(1)}, u32[]{:S(2)}, u32[]{:S(2)}) collective-permute-start(bf16[192,2048]{1,0:T(8,128)(2,1)S(1)} %add_convert_fusion.4), channel_id=1, source_target_pairs={{8,16},{16,8},{9,17},{17,9},{10,18},{18,10},{11,19},{19,11},{12,20... | collective-permute-start | bytes 2359304 | tf_op jit(solution)/shard_map/ppermute | solution.py:272
  129.4 14.5 %collective-permute-start.30 = (bf16[384,512]{1,0:T(8,128)(2,1)S(1)}, bf16[384,512]{1,0:T(8,128)(2,1)S(1)}, u32[]{:S(2)}, u32[]{:S(2)}) collective-permute-start(bf16[384,512]{1,0:T(8,128)(2,1)S(1)} %encode.7), channel_id=1, source_target_pairs={{0,2},{2,0},{4,6},{6,4},{1,3},{3,1},{5,7},{7,5},{8,10},{10,8},{12,... | collective-permute-start | bytes 1179656 | tf_op jit(solution)/shard_map/ppermute | solution.py:247
  136.8 19.6 %collective-permute-start.29 = (bf16[192,2048]{1,0:T(8,128)(2,1)S(1)}, bf16[192,2048]{1,0:T(8,128)(2,1)S(1)}, u32[]{:S(2)}, u32[]{:S(2)}) collective-permute-start(bf16[192,2048]{1,0:T(8,128)(2,1)S(1)} %get-tuple-element.159), channel_id=1, source_target_pairs={{0,8},{24,16},{1,9},{25,17},{2,10},{26,18},{3,11},{27,19},{4,12},{... | collective-permute-start | bytes 2359304 | tf_op jit(solution)/shard_map/ppermute | solution.py:264
  141.5 22.2 %collective-permute-start.26 = (bf16[192,2048]{1,0:T(8,128)(2,1)S(1)}, bf16[192,2048]{1,0:T(8,128)(2,1)S(1)}, u32[]{:S(2)}, u32[]{:S(2)}) collective-permute-start(bf16[192,2048]{1,0:T(8,128)(2,1)S(1)} %add_convert_fusion.3), channel_id=1, source_target_pairs={{8,16},{16,8},{9,17},{17,9},{10,18},{18,10},{11,19},{19,11},{12,20... | collective-permute-start | bytes 2359304 | tf_op jit(solution)/shard_map/ppermute | solution.py:272
  142.5 22.5 %collective-permute-start.28 = (bf16[192,2048]{1,0:T(8,128)(2,1)S(1)}, bf16[192,2048]{1,0:T(8,128)(2,1)S(1)}, u32[]{:S(2)}, u32[]{:S(2)}) collective-permute-start(bf16[192,2048]{1,0:T(8,128)(2,1)S(1)} %add_convert_fusion.2), channel_id=1, source_target_pairs={{8,0},{16,24},{9,1},{17,25},{10,2},{18,26},{11,3},{19,27},{12,4},{... | collective-permute-start | bytes 2359304 | tf_op jit(solution)/shard_map/ppermute | solution.py:272
  156.5 14.2 %collective-permute-start.33 = (bf16[96,2048]{1,0:T(8,128)(2,1)S(1)}, bf16[96,2048]{1,0:T(8,128)(2,1)S(1)}, u32[]{:S(2)}, u32[]{:S(2)}) collective-permute-start(bf16[96,2048]{1,0:T(8,128)(2,1)S(1)} %get-tuple-element.173), channel_id=1, source_target_pairs={{0,8},{24,16},{1,9},{25,17},{2,10},{26,18},{3,11},{27,19},{4,12},{... | collective-permute-start | bytes 1179656 | tf_op jit(solution)/shard_map/ppermute | solution.py:264
  161.1 18.0 %collective-permute-start.32 = (bf16[96,2048]{1,0:T(8,128)(2,1)S(1)}, bf16[96,2048]{1,0:T(8,128)(2,1)S(1)}, u32[]{:S(2)}, u32[]{:S(2)}) collective-permute-start(bf16[96,2048]{1,0:T(8,128)(2,1)S(1)} %get-tuple-element.172), channel_id=1, source_target_pairs={{0,8},{24,16},{1,9},{25,17},{2,10},{26,18},{3,11},{27,19},{4,12},{... | collective-permute-start | bytes 1179656 | tf_op jit(solution)/shard_map/ppermute | solution.py:264
  162.4 23.0 %collective-permute-start.36 = (bf16[96,2048]{1,0:T(8,128)(2,1)S(1)}, bf16[96,2048]{1,0:T(8,128)(2,1)S(1)}, u32[]{:S(2)}, u32[]{:S(2)}) collective-permute-start(bf16[96,2048]{1,0:T(8,128)(2,1)S(1)} %get-tuple-element.177), channel_id=1, source_target_pairs={{0,8},{24,16},{1,9},{25,17},{2,10},{26,18},{3,11},{27,19},{4,12},{... | collective-permute-start | bytes 1179656 | tf_op jit(solution)/shard_map/ppermute | solution.py:264
  163.8 25.9 %collective-permute-start.35 = (bf16[96,2048]{1,0:T(8,128)(2,1)S(1)}, bf16[96,2048]{1,0:T(8,128)(2,1)S(1)}, u32[]{:S(2)}, u32[]{:S(2)}) collective-permute-start(bf16[96,2048]{1,0:T(8,128)(2,1)S(1)} %get-tuple-element.176), channel_id=1, source_target_pairs={{0,8},{24,16},{1,9},{25,17},{2,10},{26,18},{3,11},{27,19},{4,12},{... | collective-permute-start | bytes 1179656 | tf_op jit(solution)/shard_map/ppermute | solution.py:264
  179.2 12.7 %collective-permute-start.34 = (bf16[96,2048]{1,0:T(8,128)(2,1)S(1)}, bf16[96,2048]{1,0:T(8,128)(2,1)S(1)}, u32[]{:S(2)}, u32[]{:S(2)}) collective-permute-start(bf16[96,2048]{1,0:T(8,128)(2,1)S(1)} %add_convert_fusion.9), channel_id=1, source_target_pairs={{8,16},{16,8},{9,17},{17,9},{10,18},{18,10},{11,19},{19,11},{12,20... | collective-permute-start | bytes 1179656 | tf_op jit(solution)/shard_map/ppermute | solution.py:272
  180.0 13.1 %collective-permute-start.39 = (bf16[96,2048]{1,0:T(8,128)(2,1)S(1)}, bf16[96,2048]{1,0:T(8,128)(2,1)S(1)}, u32[]{:S(2)}, u32[]{:S(2)}) collective-permute-start(bf16[96,2048]{1,0:T(8,128)(2,1)S(1)} %add_convert_fusion.8), channel_id=1, source_target_pairs={{8,0},{16,24},{9,1},{17,25},{10,2},{18,26},{11,3},{19,27},{12,4},{... | collective-permute-start | bytes 1179656 | tf_op jit(solution)/shard_map/ppermute | solution.py:272
  190.6 16.3 %collective-permute-start.41 = (bf16[96,2048]{1,0:T(8,128)(2,1)S(1)}, bf16[96,2048]{1,0:T(8,128)(2,1)S(1)}, u32[]{:S(2)}, u32[]{:S(2)}) collective-permute-start(bf16[96,2048]{1,0:T(8,128)(2,1)S(1)} %add_convert_fusion.5), channel_id=1, source_target_pairs={{8,0},{16,24},{9,1},{17,25},{10,2},{18,26},{11,3},{19,27},{12,4},{... | collective-permute-start | bytes 1179656 | tf_op jit(solution)/shard_map/ppermute | solution.py:272
  (19 other events, 174.2 us)

commit v3 on v2

--- a/solution.py
+++ b/solution.py
@@ -7,12 +7,13 @@
 
 SIXTHS = (12, 12)
 DIRECT = ''
+SPLIT = 'f'
 ORDER = (
     "x.0", "all.0", "b1.0", "x.1", "named.0", "wa1.0", "wb1.0", "b2.0", "c2.0", "setup.0", "wset.0",
-    "a1.1", "b1.1", "ena.0", "c3.0", "wc2.0", "ma.0", "b2.1", "c1.1", "dea.0", "s1.0", "wc3.0",
-    "enb.0", "c2.1", "mb.0", "wc1.1", "ena.1", "ws1.0", "c3.1", "deb.0", "s3.0", "s2.0", "wc2.1",
+    "a1.1", "b1.1", "ena.0", "c3.0", "wc2.0", "ma.0", "b2.1", "c1.1", "dea.0", "s1.0", "c2.1",
+    "wc3.0", "enb.0", "mb.0", "wc1.1", "ena.1", "ws1.0", "c3.1", "deb.0", "s3.0", "s2.0", "wc2.1",
     "ma.1", "dea.1", "s1.1", "t2.0", "wc3.1", "enf.1", "t1.0", "u1.0", "mf.1", "wxf.1", "def.1",
-    "s3p.1", "s2p.1", "s3q.1", "s2q.1", "ws1.1", "fin.0", "t2p.1", "t1p.1", "u1p.1", "t2q.1",
+    "s3p.1", "s3q.1", "s2p.1", "s2q.1", "ws1.1", "fin.0", "t2p.1", "t2q.1", "t1p.1", "u1p.1",
     "t1q.1", "u1q.1", "fin.1",
 )
 TO_MID = [(0, 1), (3, 2)]
@@ -25,16 +26,15 @@
 WSPEC = pl.BlockSpec(memory_space=pltpu.VMEM)
 VMEM = 20 << 20
 DTILE = 1024
-ONEAR = True
 
 
 def encode_kernel(slots, off, s_ref, pos, *refs):
     half = len(slots)
     at_end, at_mid = refs[:half], refs[half:2 * half]
-    wo, wp, out, xs, pre, sem = refs[2 * half:]
-    r = out.shape[0] // half
+    wo, wp, outs, (xs, pre, sem) = refs[2 * half], refs[2 * half + 1], refs[2 * half + 2:-3], refs[-3:]
+    r = xs.shape[0] // half
     top = pos.shape[2]
-    bw = out.shape[1] // top
+    bw = outs[0].shape[1] // top
     cols = wo.shape[1]
     end = s_ref[0] == 1
 
@@ -66,21 +66,26 @@
                 for b in range(2 * cols // bw):
                     base = s_ref[1] + b if b < cols // bw else s_ref[2] + b - cols // bw
                     a = jnp.where(q == base, pre[rs, b * bw:(b + 1) * bw], a)
-                out[rs, k * bw:(k + 1) * bw] = a.astype(BF)
-
-
-def decode_kernel(slots, off, count, s_ref, pos, *refs):
+                if len(outs) == 1:
+                    outs[0][rs, k * bw:(k + 1) * bw] = a.astype(BF)
+                else:
+                    outs[i][at:at + step, k * bw:(k + 1) * bw] = a.astype(BF)
+
+
+def decode_kernel(slots, off, count, split, s_ref, pos, *refs):
     parts, (bo, bp, wo, wp), outs, codes = refs[:count], refs[count:count + 4], refs[count + 4:-1], refs[-1]
     own = parts[0]
     top = pos.shape[2]
     bw = own.shape[1] // top
-    r = own.shape[0] // len(slots)
+    r = own.shape[0] if split else own.shape[0] // len(slots)
     h, width = wo.shape
     for i, slot in enumerate(slots):
         p = pos[s_ref[3 + slot], off:off + r, :]
         rs = slice(i * r, (i + 1) * r)
         wide = [jnp.broadcast_to(p[:, k:k + 1], (r, bw)) for k in range(top)]
-        tot = [sum(p_[rs, c].astype(F32) for p_ in parts)
+        mine = parts[i * count // len(slots):(i + 1) * count // len(slots)] if split else parts
+        ps = slice(0, r) if split else rs
+        tot = [sum(q[ps, c].astype(F32) for q in mine)
                for c in (slice(k * bw, (k + 1) * bw) for k in range(top))]
         for bias, base, at in ((bo, s_ref[1], 0), (bp, s_ref[2], h)):
             for b in range(h // bw):
@@ -109,16 +114,16 @@
 NEAR, FAR = pl.BlockSpec(memory_space=pltpu.VMEM), pl.BlockSpec(memory_space=pl.ANY)
 
 
-def encode(scal, pos, off, slots, at_end, at_mid, wo, wp, bw):
+def encode(scal, pos, off, slots, at_end, at_mid, wo, wp, bw, cut):
     r, width = at_end[0].shape
     cols = wo.shape[1]
     top = pos.shape[2]
     n = len(slots)
     return pl.pallas_call(
         lambda *refs: encode_kernel(slots, off, *refs),
-        out_shape=jax.ShapeDtypeStruct((n * r, top * bw), BF),
+        out_shape=[jax.ShapeDtypeStruct((n * r // cut, top * bw), BF)] * cut,
         in_specs=[pl.BlockSpec(memory_space=pltpu.SMEM), NEAR] + [FAR] * (2 * n) + [WSPEC] * 2,
-        out_specs=NEAR if ONEAR else FAR,
+        out_specs=[NEAR] * cut,
         scratch_shapes=[pltpu.VMEM((n * r, width), BF), pltpu.VMEM((n * r, 2 * cols), F32), pltpu.SemaphoreType.DMA((n,))],
         compiler_params=pltpu.CompilerParams(vmem_limit_bytes=VMEM),
         cost_estimate=pl.CostEstimate(flops=1, bytes_accessed=1, transcendentals=0),
@@ -126,12 +131,12 @@
     )(scal, pos, *at_end, *at_mid, wo, wp)
 
 
-def decode(scal, pos, off, slots, kinds, parts, bo, bp, wo, wp, cut=1):
+def decode(scal, pos, off, slots, kinds, parts, bo, bp, wo, wp, cut, split):
     n = len(slots)
-    r = parts[0].shape[0] // n
+    r = parts[0].shape[0] if split else parts[0].shape[0] // n
     half, width = wo.shape
     return pl.pallas_call(
-        lambda *refs: decode_kernel(slots, off, len(parts), *refs),
+        lambda *refs: decode_kernel(slots, off, len(parts), split, *refs),
         out_shape=[jax.ShapeDtypeStruct((r // cut, width), kind) for kind in kinds for _ in range(cut)],
         in_specs=[pl.BlockSpec(memory_space=pltpu.SMEM)] + [NEAR] * (3 + len(parts)) + [WSPEC] * 2,
         out_specs=[NEAR] * (len(kinds) * cut),
@@ -230,16 +235,22 @@
             wait(d, "b2")
             d["c3"] = pp(d["b2"], "seq", TO_END)
         elif name[:2] == "wx":
-            wait(d, *["p" + name[2] + n for n in (("d", "x", "y") if name[2] in DIRECT else ("y",))])
+            h = name[2]
+            wait(d, *(("r" + h + "x", "r" + h + "y") if h in SPLIT else ["p" + h + n for n in (("d", "x", "y") if h in DIRECT else ("y",))]))
         elif name[0] == "w":
             wait(d, name[1:])
         elif name[:2] == "en":
             h = name[2]
             ends, mids, slots, _ = GROUPS[h]
             rows = after(*[d[n] for n in ends + mids])
-            pb = encode(m["scal"], m["pos"], offs[c], slots, rows[:len(ends)], rows[len(ends):], enc_weight, m["ep"], bw)
-            mark(pb)
-            d["p" + h] = pb
+            pb = encode(m["scal"], m["pos"], offs[c], slots, rows[:len(ends)], rows[len(ends):], enc_weight, m["ep"], bw,
+                        2 if h in SPLIT else 1)
+            mark(*pb)
+            if h in SPLIT:
+                for n, p, q in zip("xy", pb, (X_TP, Y_TP)):
+                    d["q" + h + n], d["r" + h + n] = p, pp(p, "tp", q)
+                return
+            pb = d["p" + h] = pb[0]
             if h in DIRECT:
                 for n, p in (("d", FAR_TP), ("x", X_TP), ("y", Y_TP)):
                     d["p" + h + n] = pp(pb, "tp", p)
@@ -247,17 +258,28 @@
                 d["p" + h + "x"] = pp(pb, "tp", X_TP)
         elif name[0] == "m":
             h = name[1]
+            if h in SPLIT:
+                wait(d, "r" + h + "x", "r" + h + "y")
+                for n in "xy":
+                    d["q" + h + n] = (f32(d["q" + h + n]) + f32(d["r" + h + n])).astype(BF)
+                mark(d["q" + h + "x"], d["q" + h + "y"])
+                for n, q in zip("xy", (Y_TP, X_TP)):
+                    d["r" + h + n] = pp(d["q" + h + n], "tp", q)
+                return
             wait(d, "p" + h + "x")
             d["p" + h] = (f32(d["p" + h]) + f32(d["p" + h + "x"])).astype(BF)
             mark(d["p" + h])
             d["p" + h + "y"] = pp(d["p" + h], "tp", Y_TP)
         elif name[:2] == "de":
             h = name[2]
-            parts = after(*[d["p" + h + n] for n in (("", "x", "y", "d") if h in DIRECT else ("", "y"))])
+            names = ["p" + h + n for n in (("", "x", "y", "d") if h in DIRECT else ("", "y"))]
+            if h in SPLIT:
+                names = [k + h + n for n in "xy" for k in "qr"]
+            parts = after(*[d[n] for n in names])
             _, _, slots, ys = GROUPS[h]
             kinds = [F32 if n == 0 else BF for n in slots]
             out = decode(m["scal"], m["pos"], offs[c], slots, kinds, parts, m["bo"], m["bp"], dec_weight, m["dp"],
-                         len(ys) // len(slots))
+                         len(ys) // len(slots), h in SPLIT)
             mark(*out)
             d.update(zip(ys, out))
         elif name[0] == "s":

time: 210 us -> 204 us (0.971)
  waiting for transfers between devices: 91.5 us -> 85.4 us
    ppermute x4 -> x3, waiting for transfers between devices: 6.92 us -> 0.58 us  [step(): d['p' + h + 'y'] = pp(d['p' + h], 'tp', Y_TP)]
    ppermute x0 -> x4, starting transfers between devices: none -> 4.37 us  [the longest x2 2.22 us: step(): d['r' + h + n] = pp(d['q' + h + n], 'tp', q)]
    ppermute x0 -> x4, waiting for transfers between devices: none -> 4.16 us  [the longest x2 4.15 us: step(): d['r' + h + n] = pp(d['q' + h + n], 'tp', q)]
    ppermute x9, waiting for transfers between devices: 15 us -> 12.3 us  [step(): d[name] = pp(z, 'seq', ACROSS if name[0] == 't' else TO_END)]
    ppermute x4 -> x3, starting transfers between devices: 6.34 us -> 4.75 us  [step(): d['p' + h + 'y'] = pp(d['p' + h], 'tp', Y_TP)]
    ppermute x4 -> x3, starting transfers between devices: 5.94 us -> 4.67 us  [step(): d['p' + h + 'x'] = pp(pb, 'tp', X_TP)]
  transfers between devices with their start and end apart: 42 -> 44, of which waited for: 22 -> 22; matrix products, arithmetic and copies ran while one was open for 2% -> 2% of each run, Pallas kernels for 17% -> 18%
where the time goes in v3:
time: 204 us; the launch traced here: 203 us
  waiting for transfers between devices  85.4 us (42%)
  starting transfers between devices  72.6 us (36%)
  Pallas kernels  35.9 us (18%)
  other arithmetic  7.32 us (4%)
    ppermute x8, waiting for transfers between devices, step(): d[name] = pp(after(part(d, name[1], name[2:]))[0], 'seq', TO_MID)  31.1 us
    ppermute x8, starting transfers between devices, step(): d[name] = pp(after(part(d, name[1], name[2:]))[0], 'seq', TO_MID)  27.3 us
    pallas_call x4, Pallas kernels, decode(): pl.pallas_call(lambda *refs: decode_kernel(slots, off, len(parts), split,...  18.6 us
    pallas_call x4, Pallas kernels, encode(): pl.pallas_call(lambda *refs: encode_kernel(slots, off, *refs), out_shape=...  17.3 us
    ppermute x3, waiting for transfers between devices, named(): m[f'n{k}'] = pp(pos, 'seq', [(i, (i + k) % nseq) for i in range(nseq)])  13.5 us
    ppermute x9, waiting for transfers between devices, step(): d[name] = pp(z, 'seq', ACROSS if name[0] == 't' else TO_END)  12.3 us
    ppermute x1, waiting for transfers between devices, step(): d['a1'] = pp(after(d['x'])[0], 'seq', TO_MID)  8.37 us
    ppermute x9, starting transfers between devices, step(): d[name] = pp(z, 'seq', ACROSS if name[0] == 't' else TO_END)  8.04 us
  transfers between devices with their start and end apart: 44, of which 22 were waited for; matrix products, arithmetic and copies ran while one was open for 2% of the time, Pallas kernels for 18%

profile of v3, /device:TPU:0, one launch (start us, length us, event | category | flops | bytes accessed | tf_op | source)
XLA Modules:
  0.0 203.2 jit_solution(1985777024789252146)
XLA Ops:
  1.4 3.1 %collective-permute-start.3 = (bf16[192,2048]{1,0:T(8,128)(2,1)S(1)}, bf16[192,2048]{1,0:T(8,128)(2,1)}, u32[]{:S(2)}, u32[]{:S(2)}) collective-permute-start(bf16[192,2048]{1,0:T(8,128)(2,1)S(1)} %subtract_convert_fusion.1.refs_2_.refs_4_), channel_id=1, source_target_pairs={{0,8},{24,16},{8,0},{16,24},{1,9},{25,17},{9,1},{17,25},{2,10},{26... | collective-permute-start | bytes 2359304 | tf_op jit(solution)/shard_map/ppermute | solution.py:215
  6.2 3.6 %collective-permute-start = (s32[384,4]{0,1:T(4,128)S(1)}, s32[384,4]{0,1:T(4,128)S(1)}, u32[]{:S(2)}, u32[]{:S(2)}) collective-permute-start(s32[384,4]{0,1:T(4,128)S(1)} %select_reduce_fusion), channel_id=1, source_target_pairs={{0,8},{8,16},{16,24},{24,0},{1,9},{9,17},{17,25},{25,1},{2,10},{10... | collective-permute-start | bytes 18440 | tf_op jit(solution)/shard_map/ppermute | solution.py:194
  9.8 2.4 %collective-permute-start.2 = (s32[384,4]{0,1:T(4,128)S(1)}, s32[384,4]{0,1:T(4,128)S(1)}, u32[]{:S(2)}, u32[]{:S(2)}) collective-permute-start(s32[384,4]{0,1:T(4,128)S(1)} %select_reduce_fusion), channel_id=1, source_target_pairs={{0,24},{8,0},{16,8},{24,16},{1,25},{9,1},{17,9},{25,17},{2,26},{10... | collective-permute-start | bytes 18440 | tf_op jit(solution)/shard_map/ppermute | solution.py:194
  13.2 11.3 %collective-permute-done = s32[384,4]{0,1:T(4,128)S(1)} collective-permute-done((s32[384,4]{0,1:T(4,128)S(1)}, s32[384,4]{0,1:T(4,128)S(1)}, u32[]{:S(2)}, u32[]{:S(2)}) %collective-permute-start) | collective-permute-done | bytes 6176 | tf_op jit(solution)/shard_map/ppermute | solution.py:194
  24.6 2.1 %collective-permute-done.1 = s32[384,4]{0,1:T(4,128)S(1)} collective-permute-done((s32[384,4]{0,1:T(4,128)S(1)}, s32[384,4]{0,1:T(4,128)S(1)}, u32[]{:S(2)}, u32[]{:S(2)}) %collective-permute-start.1) | collective-permute-done | bytes 6176 | tf_op jit(solution)/shard_map/ppermute | solution.py:194
  31.4 2.1 %collective-permute-done.7.refs_5_.refs_7_ = f32[1,512]{1,0:T(1,128)S(1)} collective-permute-done((f32[1,512]{1,0:T(1,128)S(1)}, f32[1,512]{1,0:T(1,128)S(1)}, u32[]{:S(2)}, u32[]{:S(2)}) %collective-permute-start.7) | collective-permute-done | bytes 2080 | tf_op jit(solution)/shard_map/ppermute | solution.py:203
  35.4 4.9 %encode.4 = bf16[384,512]{1,0:T(8,128)(2,1)S(1)} custom-call(s32[7]{0:T(128)S(1)} %pad_add_fusion.1.refs_0_, s32[4,384,4]{2,1,0:T(8,128)S(1)} %copy.20.refs_1_, bf16[192,2048]{1,0:T(8,128)(2,1)S(1)} %copy-done.3, bf16[192,2048]{1,0:T(8,128)(2,1)} %collective-permute-done.3.refs_3_.refs_5_, bf16[192,2048]{1,0:T(8,128)(2,1)S(1)} %copy-done.3, ...), custom_call_target="tpu_custom_call" | custom-call | flops 1 | bytes 1 | tf_op jit(solution)/shard_map/encode/pallas_call | solution.py:122
  41.9 2.6 %collective-permute-start.12 = (bf16[192,2048]{1,0:T(8,128)(2,1)S(1)}, bf16[192,2048]{1,0:T(8,128)(2,1)S(1)}, u32[]{:S(2)}, u32[]{:S(2)}) collective-permute-start(bf16[192,2048]{1,0:T(8,128)(2,1)S(1)} %copy-done.1), channel_id=1, source_target_pairs={{0,8},{24,16},{1,9},{25,17},{2,10},{26,18},{3,11},{27,19},{4,12},{... | collective-permute-start | bytes 2359304 | tf_op jit(solution)/shard_map/ppermute | solution.py:223
  46.5 4.1 %collective-permute-done.9.refs_2_ = bf16[192,2048]{1,0:T(8,128)(2,1)} collective-permute-done((bf16[192,2048]{1,0:T(8,128)(2,1)}, bf16[192,2048]{1,0:T(8,128)(2,1)}, u32[]{:S(2)}, u32[]{:S(2)}) %collective-permute-start.9) | collective-permute-done | bytes 786464 | tf_op jit(solution)/shard_map/ppermute | solution.py:233
  53.2 8.4 %collective-permute-done.12.refs_5_ = bf16[192,2048]{1,0:T(8,128)(2,1)S(1)} collective-permute-done((bf16[192,2048]{1,0:T(8,128)(2,1)S(1)}, bf16[192,2048]{1,0:T(8,128)(2,1)S(1)}, u32[]{:S(2)}, u32[]{:S(2)}) %collective-permute-start.12) | collective-permute-done | bytes 786464 | tf_op jit(solution)/shard_map/ppermute | solution.py:223
  62.0 4.7 %decode.4 = (f32[192,2048]{1,0:T(8,128)S(1)}, bf16[192,2048]{1,0:T(8,128)(2,1)S(1)}) custom-call(s32[7]{0:T(128)S(1)} %pad_add_fusion.1.refs_0_, s32[4,384,4]{2,1,0:T(8,128)S(1)} %copy.20.refs_1_, bf16[384,512]{1,0:T(8,128)(2,1)S(1)} %add_convert_fusion.13.refs_2_, bf16[384,512]{1,0:T(8,128)(2,1)S(1)} %collective-permute-done.11.refs_3_, ...), custom_call_target="tpu_custom_call" | custom-call | flops 1 | bytes 1 | tf_op jit(solution)/shard_map/decode/pallas_call | solution.py:138
  69.3 4.8 %encode.5 = bf16[384,512]{1,0:T(8,128)(2,1)S(1)} custom-call(s32[7]{0:T(128)S(1)} %pad_add_fusion.1.refs_0_, s32[4,384,4]{2,1,0:T(8,128)S(1)} %copy.20.refs_1_, bf16[192,2048]{1,0:T(8,128)(2,1)} %collective-permute-done.9.refs_2_, bf16[192,2048]{1,0:T(8,128)(2,1)S(1)} %collective-permute-done.15.refs_3_, bf16[192,2048]{1,0:T(8,128)(2,1)} %collective-permute-done.10.refs_4_, ...), custom_call_target="tpu_custom_call" | custom-call | flops 1 | bytes 1 | tf_op jit(solution)/shard_map/encode/pallas_call | solution.py:122
  75.7 4.9 %collective-permute-start.13 = (bf16[192,2048]{1,0:T(8,128)(2,1)S(1)}, bf16[192,2048]{1,0:T(8,128)(2,1)S(1)}, u32[]{:S(2)}, u32[]{:S(2)}) collective-permute-start(bf16[192,2048]{1,0:T(8,128)(2,1)S(1)} %get-tuple-element.129), channel_id=1, source_target_pairs={{0,8},{24,16},{1,9},{25,17},{2,10},{26,18},{3,11},{27,19},{4,12},{... | collective-permute-start | bytes 2359304 | tf_op jit(solution)/shard_map/ppermute | solution.py:286
  84.7 5.7 %collective-permute-done.14.refs_3_ = bf16[192,2048]{1,0:T(8,128)(2,1)S(1)} collective-permute-done((bf16[192,2048]{1,0:T(8,128)(2,1)S(1)}, bf16[192,2048]{1,0:T(8,128)(2,1)S(1)}, u32[]{:S(2)}, u32[]{:S(2)}) %collective-permute-start.14) | collective-permute-done | bytes 786464 | tf_op jit(solution)/shard_map/ppermute | solution.py:227
  90.4 3.8 %encode.6 = bf16[384,512]{1,0:T(8,128)(2,1)S(1)} custom-call(s32[7]{0:T(128)S(1)} %pad_add_fusion.1.refs_0_, s32[4,384,4]{2,1,0:T(8,128)S(1)} %copy.20.refs_1_, bf16[192,2048]{1,0:T(8,128)(2,1)S(1)} %copy-done.1, bf16[192,2048]{1,0:T(8,128)(2,1)S(1)} %collective-permute-done.14.refs_3_, bf16[192,2048]{1,0:T(8,128)(2,1)S(1)} %copy-done.1, ...), custom_call_target="tpu_custom_call" | custom-call | flops 1 | bytes 1 | tf_op jit(solution)/shard_map/encode/pallas_call | solution.py:122
  95.8 4.7 %decode.5 = (bf16[192,2048]{1,0:T(8,128)(2,1)S(1)}, bf16[192,2048]{1,0:T(8,128)(2,1)S(1)}) custom-call(s32[7]{0:T(128)S(1)} %pad_add_fusion.1.refs_0_, s32[4,384,4]{2,1,0:T(8,128)S(1)} %copy.20.refs_1_, bf16[384,512]{1,0:T(8,128)(2,1)S(1)} %add_convert_fusion.12.refs_2_, bf16[384,512]{1,0:T(8,128)(2,1)S(1)} %collective-permute-done.18.refs_3_, ...), custom_call_target="tpu_custom_call" | custom-call | flops 1 | bytes 1 | tf_op jit(solution)/shard_map/decode/pallas_call | solution.py:138
  100.5 4.6 %collective-permute-start.23 = (bf16[192,2048]{1,0:T(8,128)(2,1)S(1)}, bf16[192,2048]{1,0:T(8,128)(2,1)S(1)}, u32[]{:S(2)}, u32[]{:S(2)}) collective-permute-start(bf16[192,2048]{1,0:T(8,128)(2,1)S(1)} %get-tuple-element.151), channel_id=1, source_target_pairs={{0,8},{24,16},{1,9},{25,17},{2,10},{26,18},{3,11},{27,19},{4,12},{... | collective-permute-start | bytes 2359304 | tf_op jit(solution)/shard_map/ppermute | solution.py:286
  108.1 4.8 %collective-permute-start.20 = (bf16[192,2048]{1,0:T(8,128)(2,1)S(1)}, bf16[192,2048]{1,0:T(8,128)(2,1)S(1)}, u32[]{:S(2)}, u32[]{:S(2)}) collective-permute-start(bf16[192,2048]{1,0:T(8,128)(2,1)S(1)} %get-tuple-element.149), channel_id=1, source_target_pairs={{0,8},{24,16},{1,9},{25,17},{2,10},{26,18},{3,11},{27,19},{4,12},{... | collective-permute-start | bytes 2359304 | tf_op jit(solution)/shard_map/ppermute | solution.py:286
  113.0 4.7 %decode.6 = (f32[192,2048]{1,0:T(8,128)S(1)}, bf16[192,2048]{1,0:T(8,128)(2,1)S(1)}) custom-call(s32[7]{0:T(128)S(1)} %pad_add_fusion.1.refs_0_, s32[4,384,4]{2,1,0:T(8,128)S(1)} %copy.20.refs_1_, bf16[384,512]{1,0:T(8,128)(2,1)S(1)} %add_convert_fusion.11.refs_2_, bf16[384,512]{1,0:T(8,128)(2,1)S(1)} %collective-permute-done.25.refs_3_, ...), custom_call_target="tpu_custom_call" | custom-call | flops 1 | bytes 1 | tf_op jit(solution)/shard_map/decode/pallas_call | solution.py:138
  117.7 5.3 %collective-permute-done.23 = bf16[192,2048]{1,0:T(8,128)(2,1)S(1)} collective-permute-done((bf16[192,2048]{1,0:T(8,128)(2,1)S(1)}, bf16[192,2048]{1,0:T(8,128)(2,1)S(1)}, u32[]{:S(2)}, u32[]{:S(2)}) %collective-permute-start.23) | collective-permute-done | bytes 786464 | tf_op jit(solution)/shard_map/ppermute | solution.py:286
  124.0 3.8 %encode.7 = (bf16[192,512]{1,0:T(8,128)(2,1)S(1)}, bf16[192,512]{1,0:T(8,128)(2,1)S(1)}) custom-call(s32[7]{0:T(128)S(1)} %pad_add_fusion.1.refs_0_, s32[4,384,4]{2,1,0:T(8,128)S(1)} %copy.20.refs_1_, bf16[192,2048]{1,0:T(8,128)(2,1)S(1)} %collective-permute-done.21.refs_2_, bf16[192,2048]{1,0:T(8,128)(2,1)S(1)} %collective-permute-done.22.refs_3_, ...), custom_call_target="tpu_custom_call" | custom-call | flops 1 | bytes 1 | tf_op jit(solution)/shard_map/encode/pallas_call | solution.py:122
  130.0 5.2 %collective-permute-done.20 = bf16[192,2048]{1,0:T(8,128)(2,1)S(1)} collective-permute-done((bf16[192,2048]{1,0:T(8,128)(2,1)S(1)}, bf16[192,2048]{1,0:T(8,128)(2,1)S(1)}, u32[]{:S(2)}, u32[]{:S(2)}) %collective-permute-start.20) | collective-permute-done | bytes 786464 | tf_op jit(solution)/shard_map/ppermute | solution.py:286
  135.2 4.4 %collective-permute-start.29 = (bf16[192,2048]{1,0:T(8,128)(2,1)S(1)}, bf16[192,2048]{1,0:T(8,128)(2,1)S(1)}, u32[]{:S(2)}, u32[]{:S(2)}) collective-permute-start(bf16[192,2048]{1,0:T(8,128)(2,1)S(1)} %get-tuple-element.167), channel_id=1, source_target_pairs={{0,8},{24,16},{1,9},{25,17},{2,10},{26,18},{3,11},{27,19},{4,12},{... | collective-permute-start | bytes 2359304 | tf_op jit(solution)/shard_map/ppermute | solution.py:286
  144.6 3.5 %collective-permute-done.33.refs_5_ = bf16[192,512]{1,0:T(8,128)(2,1)S(1)} collective-permute-done((bf16[192,512]{1,0:T(8,128)(2,1)S(1)}, bf16[192,512]{1,0:T(8,128)(2,1)S(1)}, u32[]{:S(2)}, u32[]{:S(2)}) %collective-permute-start.33) | collective-permute-done | bytes 196640 | tf_op jit(solution)/shard_map/ppermute | solution.py:267
  148.7 4.7 %decode.7 = (bf16[96,2048]{1,0:T(8,128)(2,1)S(1)}, bf16[96,2048]{1,0:T(8,128)(2,1)S(1)}, bf16[96,2048]{1,0:T(8,128)(2,1)S(1)}, bf16[96,2048]{1,0:T(8,128)(2,1)S(1)}) custom-call(s32[7]{0:T(128)S(1)} %pad_add_fusion.1.refs_0_, s32[4,384,4]{2,1,0:T(8,128)S(1)} %copy.20.refs_1_, bf16[192,512]{1,0:T(8,128)(2,1)S(1)} %add_convert_fusion.15.refs_2_, ...), custom_call_target="tpu_custom_call" | custom-call | flops 1 | bytes 1 | tf_op jit(solution)/shard_map/decode/pallas_call | solution.py:138
  153.4 4.6 %collective-permute-start.36 = (bf16[96,2048]{1,0:T(8,128)(2,1)S(1)}, bf16[96,2048]{1,0:T(8,128)(2,1)S(1)}, u32[]{:S(2)}, u32[]{:S(2)}) collective-permute-start(bf16[96,2048]{1,0:T(8,128)(2,1)S(1)} %get-tuple-element.186), channel_id=1, source_target_pairs={{0,8},{24,16},{1,9},{25,17},{2,10},{26,18},{3,11},{27,19},{4,12},{... | collective-permute-start | bytes 1179656 | tf_op jit(solution)/shard_map/ppermute | solution.py:286
  162.5 5.1 %collective-permute-done.36 = bf16[96,2048]{1,0:T(8,128)(2,1)S(1)} collective-permute-done((bf16[96,2048]{1,0:T(8,128)(2,1)S(1)}, bf16[96,2048]{1,0:T(8,128)(2,1)S(1)}, u32[]{:S(2)}, u32[]{:S(2)}) %collective-permute-start.36) | collective-permute-done | bytes 393248 | tf_op jit(solution)/shard_map/ppermute | solution.py:286
  168.4 7.6 %collective-permute-done.35 = bf16[96,2048]{1,0:T(8,128)(2,1)S(1)} collective-permute-done((bf16[96,2048]{1,0:T(8,128)(2,1)S(1)}, bf16[96,2048]{1,0:T(8,128)(2,1)S(1)}, u32[]{:S(2)}, u32[]{:S(2)}) %collective-permute-start.35) | collective-permute-done | bytes 393248 | tf_op jit(solution)/shard_map/ppermute | solution.py:286
  176.8 4.6 %collective-permute-done.34 = bf16[96,2048]{1,0:T(8,128)(2,1)S(1)} collective-permute-done((bf16[96,2048]{1,0:T(8,128)(2,1)S(1)}, bf16[96,2048]{1,0:T(8,128)(2,1)S(1)}, u32[]{:S(2)}, u32[]{:S(2)}) %collective-permute-start.34) | collective-permute-done | bytes 393248 | tf_op jit(solution)/shard_map/ppermute | solution.py:286
  182.3 3.3 %collective-permute-done.38 = bf16[96,2048]{1,0:T(8,128)(2,1)S(1)} collective-permute-done((bf16[96,2048]{1,0:T(8,128)(2,1)S(1)}, bf16[96,2048]{1,0:T(8,128)(2,1)S(1)}, u32[]{:S(2)}, u32[]{:S(2)}) %collective-permute-start.38) | collective-permute-done | bytes 393248 | tf_op jit(solution)/shard_map/ppermute | solution.py:286
  189.2 7.4 %collective-permute-done.43 = bf16[96,2048]{1,0:T(8,128)(2,1)S(1)} collective-permute-done((bf16[96,2048]{1,0:T(8,128)(2,1)S(1)}, bf16[96,2048]{1,0:T(8,128)(2,1)S(1)}, u32[]{:S(2)}, u32[]{:S(2)}) %collective-permute-start.43) | collective-permute-done | bytes 393248 | tf_op jit(solution)/shard_map/ppermute | solution.py:294
  196.5 5.0 %collective-permute-done.41 = bf16[96,2048]{1,0:T(8,128)(2,1)S(1)} collective-permute-done((bf16[96,2048]{1,0:T(8,128)(2,1)S(1)}, bf16[96,2048]{1,0:T(8,128)(2,1)S(1)}, u32[]{:S(2)}, u32[]{:S(2)}) %collective-permute-start.41) | collective-permute-done | bytes 393248 | tf_op jit(solution)/shard_map/ppermute | solution.py:294
  (106 shorter events, 50.9 us)
Async XLA Ops:
  1.4 25.3 %collective-permute-start.3 = (bf16[192,2048]{1,0:T(8,128)(2,1)S(1)}, bf16[192,2048]{1,0:T(8,128)(2,1)}, u32[]{:S(2)}, u32[]{:S(2)}) collective-permute-start(bf16[192,2048]{1,0:T(8,128)(2,1)S(1)} %subtract_convert_fusion.1.refs_2_.refs_4_), channel_id=1, source_target_pairs={{0,8},{24,16},{8,0},{16,24},{1,9},{25,17},{9,1},{17,25},{2,10},{26... | collective-permute-start | bytes 2359304 | tf_op jit(solution)/shard_map/ppermute | solution.py:215
  4.5 22.2 %collective-permute-start.4 = (bf16[192,2048]{1,0:T(8,128)(2,1)S(1)}, bf16[192,2048]{1,0:T(8,128)(2,1)}, u32[]{:S(2)}, u32[]{:S(2)}) collective-permute-start(bf16[192,2048]{1,0:T(8,128)(2,1)S(1)} %subtract_convert_fusion.1.refs_2_.refs_4_), channel_id=1, source_target_pairs={{8,16},{16,8},{9,17},{17,9},{10,18},{18,10},{11,19},{19,11},{12,20... | collective-permute-start | bytes 2359304 | tf_op jit(solution)/shard_map/ppermute | solution.py:225
  6.2 18.4 %collective-permute-start = (s32[384,4]{0,1:T(4,128)S(1)}, s32[384,4]{0,1:T(4,128)S(1)}, u32[]{:S(2)}, u32[]{:S(2)}) collective-permute-start(s32[384,4]{0,1:T(4,128)S(1)} %select_reduce_fusion), channel_id=1, source_target_pairs={{0,8},{8,16},{16,24},{24,0},{1,9},{9,17},{17,25},{25,1},{2,10},{10... | collective-permute-start | bytes 18440 | tf_op jit(solution)/shard_map/ppermute | solution.py:194
  9.8 16.9 %collective-permute-start.1 = (s32[384,4]{0,1:T(4,128)S(1)}, s32[384,4]{0,1:T(4,128)S(1)}, u32[]{:S(2)}, u32[]{:S(2)}) collective-permute-start(s32[384,4]{0,1:T(4,128)S(1)} %select_reduce_fusion), channel_id=1, source_target_pairs={{0,16},{8,24},{16,0},{24,8},{1,17},{9,25},{17,1},{25,9},{2,18},{10... | collective-permute-start | bytes 18440 | tf_op jit(solution)/shard_map/ppermute | solution.py:194
  9.8 16.9 %collective-permute-start.2 = (s32[384,4]{0,1:T(4,128)S(1)}, s32[384,4]{0,1:T(4,128)S(1)}, u32[]{:S(2)}, u32[]{:S(2)}) collective-permute-start(s32[384,4]{0,1:T(4,128)S(1)} %select_reduce_fusion), channel_id=1, source_target_pairs={{0,24},{8,0},{16,8},{24,16},{1,25},{9,1},{17,9},{25,17},{2,26},{10... | collective-permute-start | bytes 18440 | tf_op jit(solution)/shard_map/ppermute | solution.py:194
  27.3 17.9 %collective-permute-start.10 = (bf16[192,2048]{1,0:T(8,128)(2,1)}, bf16[192,2048]{1,0:T(8,128)(2,1)}, u32[]{:S(2)}, u32[]{:S(2)}) collective-permute-start(bf16[192,2048]{1,0:T(8,128)(2,1)} %collective-permute-done.3.refs_3_.refs_5_), channel_id=1, source_target_pairs={{8,16},{16,8},{9,17},{17,9},{10,18},{18,10},{11,19},{19,11},{12,20... | collective-permute-start | bytes 2359304 | tf_op jit(solution)/shard_map/ppermute | solution.py:230
  28.9 21.7 %collective-permute-start.9 = (bf16[192,2048]{1,0:T(8,128)(2,1)}, bf16[192,2048]{1,0:T(8,128)(2,1)}, u32[]{:S(2)}, u32[]{:S(2)}) collective-permute-start(bf16[192,2048]{1,0:T(8,128)(2,1)} %collective-permute-done.4.refs_5_), channel_id=1, source_target_pairs={{8,0},{16,24},{9,1},{17,25},{10,2},{18,26},{11,3},{19,27},{12,4},{... | collective-permute-start | bytes 2359304 | tf_op jit(solution)/shard_map/ppermute | solution.py:233
  40.3 11.2 %collective-permute-start.8 = (bf16[384,512]{1,0:T(8,128)(2,1)S(1)}, bf16[384,512]{1,0:T(8,128)(2,1)S(1)}, u32[]{:S(2)}, u32[]{:S(2)}) collective-permute-start(bf16[384,512]{1,0:T(8,128)(2,1)S(1)} %encode.4), channel_id=1, source_target_pairs={{0,2},{2,0},{4,6},{6,4},{1,3},{3,1},{5,7},{7,5},{8,10},{10,8},{12,... | collective-permute-start | bytes 1179656 | tf_op jit(solution)/shard_map/ppermute | solution.py:258
  41.9 19.7 %collective-permute-start.12 = (bf16[192,2048]{1,0:T(8,128)(2,1)S(1)}, bf16[192,2048]{1,0:T(8,128)(2,1)S(1)}, u32[]{:S(2)}, u32[]{:S(2)}) collective-permute-start(bf16[192,2048]{1,0:T(8,128)(2,1)S(1)} %copy-done.1), channel_id=1, source_target_pairs={{0,8},{24,16},{1,9},{25,17},{2,10},{26,18},{3,11},{27,19},{4,12},{... | collective-permute-start | bytes 2359304 | tf_op jit(solution)/shard_map/ppermute | solution.py:223
  44.5 22.2 %collective-permute-start.16 = (bf16[192,2048]{1,0:T(8,128)(2,1)S(1)}, bf16[192,2048]{1,0:T(8,128)(2,1)S(1)}, u32[]{:S(2)}, u32[]{:S(2)}) collective-permute-start(bf16[192,2048]{1,0:T(8,128)(2,1)S(1)} %copy-done.1), channel_id=1, source_target_pairs={{8,16},{16,8},{9,17},{17,9},{10,18},{18,10},{11,19},{19,11},{12,20... | collective-permute-start | bytes 2359304 | tf_op jit(solution)/shard_map/ppermute | solution.py:225
  45.2 22.8 %collective-permute-start.15 = (bf16[192,2048]{1,0:T(8,128)(2,1)}, bf16[192,2048]{1,0:T(8,128)(2,1)S(1)}, u32[]{:S(2)}, u32[]{:S(2)}) collective-permute-start(bf16[192,2048]{1,0:T(8,128)(2,1)} %collective-permute-done.10.refs_4_), channel_id=1, source_target_pairs={{8,0},{16,24},{9,1},{17,25},{10,2},{18,26},{11,3},{19,27},{12,4},{... | collective-permute-start | bytes 2359304 | tf_op jit(solution)/shard_map/ppermute | solution.py:236
  68.1 22.4 %collective-permute-start.14 = (bf16[192,2048]{1,0:T(8,128)(2,1)S(1)}, bf16[192,2048]{1,0:T(8,128)(2,1)S(1)}, u32[]{:S(2)}, u32[]{:S(2)}) collective-permute-start(bf16[192,2048]{1,0:T(8,128)(2,1)S(1)} %copy-done.1), channel_id=1, source_target_pairs={{8,0},{16,24},{9,1},{17,25},{10,2},{18,26},{11,3},{19,27},{12,4},{... | collective-permute-start | bytes 2359304 | tf_op jit(solution)/shard_map/ppermute | solution.py:227
  75.7 20.1 %collective-permute-start.13 = (bf16[192,2048]{1,0:T(8,128)(2,1)S(1)}, bf16[192,2048]{1,0:T(8,128)(2,1)S(1)}, u32[]{:S(2)}, u32[]{:S(2)}) collective-permute-start(bf16[192,2048]{1,0:T(8,128)(2,1)S(1)} %get-tuple-element.129), channel_id=1, source_target_pairs={{0,8},{24,16},{1,9},{25,17},{2,10},{26,18},{3,11},{27,19},{4,12},{... | collective-permute-start | bytes 2359304 | tf_op jit(solution)/shard_map/ppermute | solution.py:286
  80.6 15.2 %collective-permute-start.19 = (bf16[192,2048]{1,0:T(8,128)(2,1)S(1)}, bf16[192,2048]{1,0:T(8,128)(2,1)S(1)}, u32[]{:S(2)}, u32[]{:S(2)}) collective-permute-start(bf16[192,2048]{1,0:T(8,128)(2,1)S(1)} %collective-permute-done.12.refs_5_), channel_id=1, source_target_pairs={{8,16},{16,8},{9,17},{17,9},{10,18},{18,10},{11,19},{19,11},{12,20... | collective-permute-start | bytes 2359304 | tf_op jit(solution)/shard_map/ppermute | solution.py:230
  81.3 23.8 %collective-permute-start.21 = (bf16[192,2048]{1,0:T(8,128)(2,1)S(1)}, bf16[192,2048]{1,0:T(8,128)(2,1)S(1)}, u32[]{:S(2)}, u32[]{:S(2)}) collective-permute-start(bf16[192,2048]{1,0:T(8,128)(2,1)S(1)} %collective-permute-done.16.refs_5_), channel_id=1, source_target_pairs={{8,0},{16,24},{9,1},{17,25},{10,2},{18,26},{11,3},{19,27},{12,4},{... | collective-permute-start | bytes 2359304 | tf_op jit(solution)/shard_map/ppermute | solution.py:233
  83.1 12.7 %collective-permute-start.18 = (bf16[384,512]{1,0:T(8,128)(2,1)S(1)}, bf16[384,512]{1,0:T(8,128)(2,1)S(1)}, u32[]{:S(2)}, u32[]{:S(2)}) collective-permute-start(bf16[384,512]{1,0:T(8,128)(2,1)S(1)} %add_convert_fusion.12.refs_2_), channel_id=1, source_target_pairs={{0,4},{4,0},{2,6},{6,2},{1,5},{5,1},{3,7},{7,3},{8,12},{12,8},{10,... | collective-permute-start | bytes 1179656 | tf_op jit(solution)/shard_map/ppermute | solution.py:272
  94.2 10.9 %collective-permute-start.24 = (bf16[384,512]{1,0:T(8,128)(2,1)S(1)}, bf16[384,512]{1,0:T(8,128)(2,1)S(1)}, u32[]{:S(2)}, u32[]{:S(2)}) collective-permute-start(bf16[384,512]{1,0:T(8,128)(2,1)S(1)} %encode.6), channel_id=1, source_target_pairs={{0,2},{2,0},{4,6},{6,4},{1,3},{3,1},{5,7},{7,5},{8,10},{10,8},{12,... | collective-permute-start | bytes 1179656 | tf_op jit(solution)/shard_map/ppermute | solution.py:258
  100.5 22.5 %collective-permute-start.23 = (bf16[192,2048]{1,0:T(8,128)(2,1)S(1)}, bf16[192,2048]{1,0:T(8,128)(2,1)S(1)}, u32[]{:S(2)}, u32[]{:S(2)}) collective-permute-start(bf16[192,2048]{1,0:T(8,128)(2,1)S(1)} %get-tuple-element.151), channel_id=1, source_target_pairs={{0,8},{24,16},{1,9},{25,17},{2,10},{26,18},{3,11},{27,19},{4,12},{... | collective-permute-start | bytes 2359304 | tf_op jit(solution)/shard_map/ppermute | solution.py:286
  106.8 17.2 %collective-permute-start.22 = (bf16[192,2048]{1,0:T(8,128)(2,1)S(1)}, bf16[192,2048]{1,0:T(8,128)(2,1)S(1)}, u32[]{:S(2)}, u32[]{:S(2)}) collective-permute-start(bf16[192,2048]{1,0:T(8,128)(2,1)S(1)} %collective-permute-done.19.refs_4_), channel_id=1, source_target_pairs={{8,0},{16,24},{9,1},{17,25},{10,2},{18,26},{11,3},{19,27},{12,4},{... | collective-permute-start | bytes 2359304 | tf_op jit(solution)/shard_map/ppermute | solution.py:236
  108.1 27.1 %collective-permute-start.20 = (bf16[192,2048]{1,0:T(8,128)(2,1)S(1)}, bf16[192,2048]{1,0:T(8,128)(2,1)S(1)}, u32[]{:S(2)}, u32[]{:S(2)}) collective-permute-start(bf16[192,2048]{1,0:T(8,128)(2,1)S(1)} %get-tuple-element.149), channel_id=1, source_target_pairs={{0,8},{24,16},{1,9},{25,17},{2,10},{26,18},{3,11},{27,19},{4,12},{... | collective-permute-start | bytes 2359304 | tf_op jit(solution)/shard_map/ppermute | solution.py:286
  123.3 17.4 %collective-permute-start.27 = (bf16[192,2048]{1,0:T(8,128)(2,1)S(1)}, bf16[192,2048]{1,0:T(8,128)(2,1)S(1)}, u32[]{:S(2)}, u32[]{:S(2)}) collective-permute-start(bf16[192,2048]{1,0:T(8,128)(2,1)S(1)} %add_convert_fusion.4), channel_id=1, source_target_pairs={{8,16},{16,8},{9,17},{17,9},{10,18},{18,10},{11,19},{19,11},{12,20... | collective-permute-start | bytes 2359304 | tf_op jit(solution)/shard_map/ppermute | solution.py:294
  127.8 14.4 %collective-permute-start.30 = (bf16[192,512]{1,0:T(8,128)(2,1)S(1)}, bf16[192,512]{1,0:T(8,128)(2,1)S(1)}, u32[]{:S(2)}, u32[]{:S(2)}) collective-permute-start(bf16[192,512]{1,0:T(8,128)(2,1)S(1)} %get-tuple-element.163), channel_id=1, source_target_pairs={{0,2},{2,0},{4,6},{6,4},{1,3},{3,1},{5,7},{7,5},{8,10},{10,8},{12,... | collective-permute-start | bytes 589832 | tf_op jit(solution)/shard_map/ppermute | solution.py:251
  128.9 13.4 %collective-permute-start.31 = (bf16[192,512]{1,0:T(8,128)(2,1)S(1)}, bf16[192,512]{1,0:T(8,128)(2,1)S(1)}, u32[]{:S(2)}, u32[]{:S(2)}) collective-permute-start(bf16[192,512]{1,0:T(8,128)(2,1)S(1)} %get-tuple-element.164), channel_id=1, source_target_pairs={{0,4},{4,0},{2,6},{6,2},{1,5},{5,1},{3,7},{7,3},{8,12},{12,8},{10,... | collective-permute-start | bytes 589832 | tf_op jit(solution)/shard_map/ppermute | solution.py:251
  135.2 18.2 %collective-permute-start.29 = (bf16[192,2048]{1,0:T(8,128)(2,1)S(1)}, bf16[192,2048]{1,0:T(8,128)(2,1)S(1)}, u32[]{:S(2)}, u32[]{:S(2)}) collective-permute-start(bf16[192,2048]{1,0:T(8,128)(2,1)S(1)} %get-tuple-element.167), channel_id=1, source_target_pairs={{0,8},{24,16},{1,9},{25,17},{2,10},{26,18},{3,11},{27,19},{4,12},{... | collective-permute-start | bytes 2359304 | tf_op jit(solution)/shard_map/ppermute | solution.py:286
  139.9 20.8 %collective-permute-start.26 = (bf16[192,2048]{1,0:T(8,128)(2,1)S(1)}, bf16[192,2048]{1,0:T(8,128)(2,1)S(1)}, u32[]{:S(2)}, u32[]{:S(2)}) collective-permute-start(bf16[192,2048]{1,0:T(8,128)(2,1)S(1)} %add_convert_fusion.3), channel_id=1, source_target_pairs={{8,16},{16,8},{9,17},{17,9},{10,18},{18,10},{11,19},{19,11},{12,20... | collective-permute-start | bytes 2359304 | tf_op jit(solution)/shard_map/ppermute | solution.py:294
  140.9 21.1 %collective-permute-start.28 = (bf16[192,2048]{1,0:T(8,128)(2,1)S(1)}, bf16[192,2048]{1,0:T(8,128)(2,1)S(1)}, u32[]{:S(2)}, u32[]{:S(2)}) collective-permute-start(bf16[192,2048]{1,0:T(8,128)(2,1)S(1)} %add_convert_fusion.2), channel_id=1, source_target_pairs={{8,0},{16,24},{9,1},{17,25},{10,2},{18,26},{11,3},{19,27},{12,4},{... | collective-permute-start | bytes 2359304 | tf_op jit(solution)/shard_map/ppermute | solution.py:294
  153.4 14.2 %collective-permute-start.36 = (bf16[96,2048]{1,0:T(8,128)(2,1)S(1)}, bf16[96,2048]{1,0:T(8,128)(2,1)S(1)}, u32[]{:S(2)}, u32[]{:S(2)}) collective-permute-start(bf16[96,2048]{1,0:T(8,128)(2,1)S(1)} %get-tuple-element.186), channel_id=1, source_target_pairs={{0,8},{24,16},{1,9},{25,17},{2,10},{26,18},{3,11},{27,19},{4,12},{... | collective-permute-start | bytes 1179656 | tf_op jit(solution)/shard_map/ppermute | solution.py:286
  158.0 18.0 %collective-permute-start.35 = (bf16[96,2048]{1,0:T(8,128)(2,1)S(1)}, bf16[96,2048]{1,0:T(8,128)(2,1)S(1)}, u32[]{:S(2)}, u32[]{:S(2)}) collective-permute-start(bf16[96,2048]{1,0:T(8,128)(2,1)S(1)} %get-tuple-element.185), channel_id=1, source_target_pairs={{0,8},{24,16},{1,9},{25,17},{2,10},{26,18},{3,11},{27,19},{4,12},{... | collective-permute-start | bytes 1179656 | tf_op jit(solution)/shard_map/ppermute | solution.py:286
  159.4 22.1 %collective-permute-start.34 = (bf16[96,2048]{1,0:T(8,128)(2,1)S(1)}, bf16[96,2048]{1,0:T(8,128)(2,1)S(1)}, u32[]{:S(2)}, u32[]{:S(2)}) collective-permute-start(bf16[96,2048]{1,0:T(8,128)(2,1)S(1)} %get-tuple-element.184), channel_id=1, source_target_pairs={{0,8},{24,16},{1,9},{25,17},{2,10},{26,18},{3,11},{27,19},{4,12},{... | collective-permute-start | bytes 1179656 | tf_op jit(solution)/shard_map/ppermute | solution.py:286
  160.7 24.9 %collective-permute-start.38 = (bf16[96,2048]{1,0:T(8,128)(2,1)S(1)}, bf16[96,2048]{1,0:T(8,128)(2,1)S(1)}, u32[]{:S(2)}, u32[]{:S(2)}) collective-permute-start(bf16[96,2048]{1,0:T(8,128)(2,1)S(1)} %get-tuple-element.190), channel_id=1, source_target_pairs={{0,8},{24,16},{1,9},{25,17},{2,10},{26,18},{3,11},{27,19},{4,12},{... | collective-permute-start | bytes 1179656 | tf_op jit(solution)/shard_map/ppermute | solution.py:286
  167.7 14.5 %collective-permute-start.39 = (bf16[96,2048]{1,0:T(8,128)(2,1)S(1)}, bf16[96,2048]{1,0:T(8,128)(2,1)S(1)}, u32[]{:S(2)}, u32[]{:S(2)}) collective-permute-start(bf16[96,2048]{1,0:T(8,128)(2,1)S(1)} %add_convert_fusion.10), channel_id=1, source_target_pairs={{8,16},{16,8},{9,17},{17,9},{10,18},{18,10},{11,19},{19,11},{12,20... | collective-permute-start | bytes 1179656 | tf_op jit(solution)/shard_map/ppermute | solution.py:294
  187.8 13.6 %collective-permute-start.41 = (bf16[96,2048]{1,0:T(8,128)(2,1)S(1)}, bf16[96,2048]{1,0:T(8,128)(2,1)S(1)}, u32[]{:S(2)}, u32[]{:S(2)}) collective-permute-start(bf16[96,2048]{1,0:T(8,128)(2,1)S(1)} %add_convert_fusion.7), channel_id=1, source_target_pairs={{8,0},{16,24},{9,1},{17,25},{10,2},{18,26},{11,3},{19,27},{12,4},{... | collective-permute-start | bytes 1179656 | tf_op jit(solution)/shard_map/ppermute | solution.py:294
  (21 other events, 198.0 us)
